TPU v7x, 256 devices: a whole 4x4x8 slice. The times are simulated.
256 devices in a mesh: wrap: 16 (over x, y_hi, core), inst: 16 (over y_lo, z).
Axes of the slice: x: 4, y: 4 (y_hi: 2, y_lo: 2; y = y_hi * 2 + y_lo), z: 8, core: 2. Of those that a mesh axis runs over, the one named last changes fastest.
Arguments:
- state: float32 [32, 6, 8, 512, 128], P('inst', None, None, 'wrap'), may hold values from -0.8 to 3.3, as said below
- metrics: float32 [3, 3, 8, 512, 128], P(None, None, None, 'wrap'), may hold values from -3 to 3
- volume: float32 [8, 512, 128], P(None, 'wrap'), may hold values from 0.5 to 2
Outputs:
- residual: float32 [32, 6, 8, 512, 128], P('inst', None, None, 'wrap')
Inputs may be any that keep to these rules, and one draw needn't show every extreme that they name: Every instance and cell holds a physical state: density from 0.7 to 1.3, speed below 1.1, pressure from 0.5 to 1.0, density times turbulence variable from 0.035 to 2.6.
All inputs are finite; a program needn't handle non-finite values.
Results may differ from a plain program's by a relative error of at most 0.00018.
Values sent between devices are 32-bit elements; how exact they have to be, the bound alone decides.
No kernel may reach another device: no remote copies, remote signals or barrier semaphores. Data moves between devices by JAX's collectives and lax.ppermute only.
A program may use at most 128 MiB of HBM per device.

v0:
```python
import math

import jax
import jax.numpy as jnp
from jax import lax
from jax.sharding import PartitionSpec as P

NT = 32


dissipation = 0.03125
viscosity = 0.2
frequency = 0.25


def padded_2(cells, sides, width):
    for axis, dim in sides:
        count = lax.axis_size(axis)
        head = lax.slice_in_dim(cells, 0, width, axis=dim)
        tail = lax.slice_in_dim(cells, cells.shape[dim] - width, cells.shape[dim], axis=dim)
        cells = jnp.concatenate(
            [
                lax.ppermute(tail, axis, [(i, (i + 1) % count) for i in range(count)]),
                cells,
                lax.ppermute(head, axis, [((i + 1) % count, i) for i in range(count)]),
            ],
            axis=dim,
        )
    return cells


def spectral_table(table_size):
    index_rows = jnp.arange(table_size, dtype=jnp.int32)
    distance = index_rows[:, None] - index_rows[None, :]
    signs = jnp.where(distance % 2 == 0, 1.0, -1.0).astype(jnp.float32)
    safe = jnp.where(distance == 0, 1, distance).astype(jnp.float32)
    tangent = jnp.tan(math.pi / table_size * safe)
    return jnp.where(distance == 0, 0.0, 0.5 * signs / tangent)


def take_range(array, first, last, axis_from_end):
    return lax.slice_in_dim(array, first, last, axis=array.ndim + axis_from_end)


def edge_pad(array, width, axis_from_end):
    pad_widths = [(0, 0)] * array.ndim
    pad_widths[array.ndim + axis_from_end] = (width, width)
    return jnp.pad(array, pad_widths, mode="edge")


def state_flux(field, normals):
    density = field[..., 0, :, :, :]
    momentum = field[..., 1:4, :, :, :]
    velocity = momentum / density[..., None, :, :, :]
    normal_speed = jnp.sum(velocity * normals, axis=-4)
    pressure = 0.4 * (field[..., 4, :, :, :] - 0.5 * jnp.sum(momentum * velocity, axis=-4))
    sound_speed = jnp.sqrt(1.4 * pressure / density)
    face_area = jnp.sqrt(jnp.sum(normals * normals, axis=0))
    radius = jnp.abs(normal_speed) + sound_speed * face_area
    cell_flux = jnp.concatenate(
        [
            (density * normal_speed)[..., None, :, :, :],
            momentum * normal_speed[..., None, :, :, :] + pressure[..., None, :, :, :] * normals,
            ((field[..., 4, :, :, :] + pressure) * normal_speed)[..., None, :, :, :],
            (field[..., 5, :, :, :] * normal_speed)[..., None, :, :, :],
        ],
        axis=-4,
    )
    return (cell_flux, radius)


def direction_residual(padded, metric_padded, axis_from_end):
    length = padded.shape[padded.ndim + axis_from_end] - 4
    inner_cells = take_range(padded, 1, length + 3, axis_from_end)
    cell_flux, radius = state_flux(inner_cells, metric_padded)
    central = 0.5 * (
        take_range(cell_flux, 0, length + 1, axis_from_end)
        + take_range(cell_flux, 1, length + 2, axis_from_end)
    )
    radius_face = 0.5 * (
        take_range(radius, 0, length + 1, axis_from_end)
        + take_range(radius, 1, length + 2, axis_from_end)
    )
    fourth = (
        take_range(padded, 3, length + 4, axis_from_end)
        - 3.0 * take_range(padded, 2, length + 3, axis_from_end)
        + 3.0 * take_range(padded, 1, length + 2, axis_from_end)
        - take_range(padded, 0, length + 1, axis_from_end)
    )
    face_flux = central - dissipation * radius_face[..., None, :, :, :] * fourth
    return take_range(face_flux, 1, length + 1, axis_from_end) - take_range(
        face_flux, 0, length, axis_from_end
    )


def spatial(field, field_wrap, metric_wrap, metrics, volume):
    convective = direction_residual(field_wrap, metric_wrap, -2)
    convective = convective + direction_residual(
        edge_pad(field, 2, -1), edge_pad(metrics[1], 1, -1), -1
    )
    convective = convective + direction_residual(
        edge_pad(field, 2, -3), edge_pad(metrics[2], 1, -3), -3
    )
    length = field.shape[-1]
    padded_j = edge_pad(field, 1, -1)
    geometry = edge_pad(jnp.sum(metrics[1] * metrics[1], axis=0) / volume, 1, -1)
    coefficient = viscosity * (1.0 + padded_j[..., 5, :, :, :]) * geometry
    face_coef = 0.5 * (
        take_range(coefficient, 0, length + 1, -1) + take_range(coefficient, 1, length + 2, -1)
    )
    difference = take_range(padded_j, 1, length + 2, -1) - take_range(padded_j, 0, length + 1, -1)
    face_term = face_coef[..., None, :, :, :] * difference
    var_mask = jnp.array([0.0, 1.0, 1.0, 1.0, 1.0, 1.0], jnp.float32)[:, None, None, None]
    viscous = (
        take_range(face_term, 1, length + 1, -1) - take_range(face_term, 0, length, -1)
    ) * var_mask
    return convective - viscous


def body(state, metrics, volume):
    derivative = spectral_table(NT)
    inst_count = state.shape[0]
    offset = lax.axis_index("inst") * inst_count
    state_wrap = padded_2(state, (("wrap", 3),), 2)
    metric_wrap = padded_2(metrics[0], (("wrap", 2),), 1)
    local_terms = spatial(state, state_wrap, metric_wrap, metrics, volume)
    own_rows = lax.dynamic_slice_in_dim(derivative, offset, inst_count, 0)
    time_term = jnp.einsum(
        "nm,mvkij->nvkij",
        own_rows,
        lax.all_gather(state, "inst", axis=0, tiled=True),
        precision=lax.Precision.HIGHEST,
    )
    return local_terms + frequency * volume * time_term


def solution(mesh):
    in_specs = (
        P("inst", None, None, "wrap", None),
        P(None, None, None, "wrap", None),
        P(None, "wrap", None),
    )
    out_specs = P("inst", None, None, "wrap", None)
    return jax.shard_map(body, mesh=mesh, in_specs=in_specs, out_specs=out_specs, check_vma=False)
```

profile of v0, /device:TPU:225, one launch (start us, length us, event | category | flops | bytes accessed | tf_op | source)
XLA Modules:
  0.0 335.2 jit_solution(13711950962039040890)
XLA Ops:
  7.9 1.4 copy.53
  10.0 3.5 %collective-permute-start = (f32[2,6,8,2,128]{4,0,3,2,1:T(2,128)}, f32[2,6,8,2,128]{4,0,3,2,1:T(2,128)}, u32[]{:S(2)}, u32[]{:S(2)}) collective-permute-start(f32[2,6,8,2,128]{4,0,3,2,1:T(2,128)} %get-tuple-element.25), channel_id=1, source_target_pairs={{0,16},{16,32},{32,48},{48,64},{64,80},{80,96},{96,112},{112,128},... | collective-permute-start | bytes 294920 | tf_op jit(solution)/shard_map/ppermute | solution.py:23
  15.7 3.2 collective-permute-start.2
  19.0 3.4 %fusion.75 = (f32[2,6,8,32,1]{4,0,3,2,1:T(2,128)}, f32[2,6,8,32,1]{4,0,3,2,1:T(2,128)}) fusion(f32[2,6,8,32,128]{4,0,3,2,1:T(2,128)S(1)} %copy.53), kind=kLoop, calls=%fused_computation.170 | loop fusion | bytes 49152 | tf_op jit(solution)/shard_map/jit(_pad)/slice | solution.py:48
  22.4 11.1 %copy.80 = f32[2,6,8,32,1]{0,3,2,1,4:T(8,128)} copy(f32[2,6,8,32,1]{4,0,3,2,1:T(2,128)} %get-tuple-element.30) | data formatting | bytes 24576 | tf_op jit(solution)/shard_map/jit(_pad)/slice | solution.py:48
  33.6 2.8 copy.72
  36.3 11.0 %copy.81 = f32[2,6,8,32,1]{0,3,2,1,4:T(8,128)} copy(f32[2,6,8,32,1]{4,0,3,2,1:T(2,128)} %get-tuple-element.31) | data formatting | bytes 24576 | tf_op jit(solution)/shard_map/jit(_pad)/slice | solution.py:48
  47.3 1.7 copy.73
  55.1 1.9 reshape.86
  57.0 1.9 reshape.87
  60.1 1.3 pad_maximum_fusion.5
  63.7 5.9 %pad_maximum_fusion.3 = f32[2,6,8,32,132]{4,0,3,2,1:T(2,128)S(1)} fusion(f32[2,6,8,32,2]{4,0,3,2,1:T(2,128)S(1)} %reshape.87, f32[2,6,8,32,128]{4,0,3,2,1:T(2,128)S(1)} %copy.53, f32[2,6,8,32,2]{4,0,3,2,1:T(2,128)S(1)} %reshape.86), kind=kLoop, calls=%fused_computation.15 | loop fusion | flops 811008 | bytes 3244032 | tf_op jit(solution)/shard_map/jit(_pad)/concatenate | solution.py:48
  69.6 2.9 multiply_reduce_fusion
  72.5 2.2 multiply_add_fusion.3
  78.2 2.2 fusion.47
  80.4 1.8 multiply_add_fusion
  82.2 1.9 pad_maximum_fusion.4
  84.1 9.0 %fusion.18 = f32[2,6,9,32,128]{4,0,3,2,1:T(2,128)} fusion(f32[2,6,10,32,128]{4,0,3,2,1:T(2,128)S(1)} %pad_maximum_fusion.6, f32[2,6,8,32,128]{4,0,3,2,1:T(2,128)S(1)} %copy.53, f32[2,6,2,32,128]{4,0,3,2,1:T(2,128)S(1)} %reshape.88, f32[2,6,2,32,128]{4,0,3,2,1:T(2,128)S(1)} %reshape.89, f32[2,9,32,128]{3,0,2,1:T(2,128)S(1)} %fusion.42), kind=kLoop, calls=%fused_computation.34 | loop fusion | flops 5750784 | bytes 7962624 | tf_op jit(solution)/shard_map/sub | solution.py:90
  93.1 21.6 %fusion.9 = (f32[2,6,8,32,129]{4,0,3,2,1:T(2,128)}, f32[2,6,8,32,129]{4,0,3,2,1:T(2,128)}) fusion(f32[2,6,8,32,130]{4,0,3,2,1:T(2,128)S(1)} %pad_maximum_fusion.4, f32[2,6,8,32,128]{4,0,3,2,1:T(2,128)S(1)} %copy.53, f32[2,6,8,32,2]{4,0,3,2,1:T(2,128)S(1)} %reshape.86, f32[2,6,8,32,2]{4,0,3,2,1:T(2,128)S(1)} %reshape.87, f32[2,8,32,129]{3,0,2,1:T(2,128)S(1)} %fusion.35, ...), kind=kLoop, calls=%fused_computation.14 | loop fusion | flops 6736896 | bytes 8515584 | tf_op jit(solution)/shard_map/sub | solution.py:90
  115.3 161.4 %collective-permute-done.3 = f32[3,8,1,128]{3,2,1,0:T(1,128)} collective-permute-done((f32[3,8,1,128]{3,2,1,0:T(1,128)}, f32[3,8,1,128]{3,2,1,0:T(1,128)}, u32[]{:S(2)}, u32[]{:S(2)}) %collective-permute-start.3) | collective-permute-done | bytes 12320 | tf_op jit(solution)/shard_map/ppermute | solution.py:25
  278.5 2.3 constant_dynamic-update-slice_fusion.1
  285.6 2.8 fusion.20
  288.5 38.3 %fusion.26 = f32[2,6,8,32,128]{4,0,3,2,1:T(2,128)S(1)} fusion(f32[2,6,8,32,129]{4,0,3,2,1:T(2,128)} %get-tuple-element.27, f32[2,6,9,32,128]{4,0,3,2,1:T(2,128)} %fusion.18, f32[2,6,8,32,129]{4,0,3,2,1:T(2,128)} %get-tuple-element.26, f32[2,6,8,33,128]{4,0,3,2,1:T(2,128)S(1)} %fusion.20, f32[32,6,8,32,128]{4,3,2,1,0:T(8,128)} %all-gather.2.cloned.1.call-done, ...), kind=kOutput, calls=%fused_computation.48 | convolution fusion | flops 154927680 | bytes 39457284 | tf_op jit(solution)/shard_map/nm,mvkij->nvkij/dot_general | solution.py:128
  326.8 1.4 copy.78
  (78 shorter events, 24.2 us)
Async XLA Ops:
  6.5 1.4 copy-start
  6.5 281.9 %all-gather.2.cloned.1.call-start = ((), (), s32[]{:S(2)}) async-start(), calls=%async_computation | async-start | bytes 26738688 | tf_op jit(solution)/shard_map/all_gather | solution.py:131
  7.9 5.6 %copy-start.6 = (f32[3,3,8,32,128]{4,3,2,1,0:T(8,128)S(1)}, f32[3,3,8,32,128]{4,3,2,1,0:T(8,128)}, u32[]{:S(2)}) copy-start(f32[3,3,8,32,128]{4,3,2,1,0:T(8,128)} %param.5) | copy-start | bytes 3538948
  10.0 267.5 %collective-permute-start = (f32[2,6,8,2,128]{4,0,3,2,1:T(2,128)}, f32[2,6,8,2,128]{4,0,3,2,1:T(2,128)}, u32[]{:S(2)}, u32[]{:S(2)}) collective-permute-start(f32[2,6,8,2,128]{4,0,3,2,1:T(2,128)} %get-tuple-element.25), channel_id=1, source_target_pairs={{0,16},{16,32},{32,48},{48,64},{64,80},{80,96},{96,112},{112,128},... | collective-permute-start | bytes 294920 | tf_op jit(solution)/shard_map/ppermute | solution.py:23
  13.5 267.3 %collective-permute-start.1 = (f32[2,6,8,2,128]{4,0,3,2,1:T(2,128)}, f32[2,6,8,2,128]{4,0,3,2,1:T(2,128)}, u32[]{:S(2)}, u32[]{:S(2)}) collective-permute-start(f32[2,6,8,2,128]{4,0,3,2,1:T(2,128)} %get-tuple-element.24), channel_id=1, source_target_pairs={{16,0},{32,16},{48,32},{64,48},{80,64},{96,80},{112,96},{128,112},... | collective-permute-start | bytes 294920 | tf_op jit(solution)/shard_map/ppermute | solution.py:25
  14.4 0.8 copy-start.8
  15.7 99.6 %collective-permute-start.2 = (f32[3,8,1,128]{3,2,1,0:T(1,128)}, f32[3,8,1,128]{3,2,1,0:T(1,128)}, u32[]{:S(2)}, u32[]{:S(2)}) collective-permute-start(f32[3,8,1,128]{3,2,1,0:T(1,128)} %get-tuple-element.45), channel_id=1, source_target_pairs={{0,16},{16,32},{32,48},{48,64},{64,80},{80,96},{96,112},{112,128},... | collective-permute-start | bytes 36872 | tf_op jit(solution)/shard_map/ppermute | solution.py:23
  19.0 257.7 %collective-permute-start.3 = (f32[3,8,1,128]{3,2,1,0:T(1,128)}, f32[3,8,1,128]{3,2,1,0:T(1,128)}, u32[]{:S(2)}, u32[]{:S(2)}) collective-permute-start(f32[3,8,1,128]{3,2,1,0:T(1,128)} %get-tuple-element.46), channel_id=1, source_target_pairs={{16,0},{32,16},{48,32},{64,48},{80,64},{96,80},{112,96},{128,112},... | collective-permute-start | bytes 36872 | tf_op jit(solution)/shard_map/ppermute | solution.py:25
  47.3 2.0 copy-start.7
  49.7 1.6 copy-start.11
  50.1 2.2 copy-start.3
  54.0 1.1 copy-start.4
  54.3 2.8 copy-start.5
  84.1 9.0 %copy-start.1 = (f32[2,6,8,32,1]{4,0,3,2,1:T(2,128)S(1)}, f32[2,6,8,32,1]{4,0,3,2,1:T(2,128)}, u32[]{:S(2)}) copy-start(f32[2,6,8,32,1]{4,0,3,2,1:T(2,128)} %get-tuple-element.30) | copy-start | bytes 36868
  84.1 9.0 %copy-start.2 = (f32[2,6,8,32,1]{4,0,3,2,1:T(2,128)S(1)}, f32[2,6,8,32,1]{4,0,3,2,1:T(2,128)}, u32[]{:S(2)}) copy-start(f32[2,6,8,32,1]{4,0,3,2,1:T(2,128)} %get-tuple-element.31) | copy-start | bytes 36868
  93.1 183.6 %copy-start.9 = (f32[3,8,32,128]{3,2,1,0:T(8,128)S(1)}, f32[3,8,32,128]{3,2,1,0:T(8,128)}, u32[]{:S(2)}) copy-start(f32[3,8,32,128]{3,2,1,0:T(8,128)} %copy-done.8) | copy-start | bytes 1179652
  285.6 2.9 copy-start.10
  285.6 2.9 copy-start.12
Sparse Core Ops, SparseCore 0:
  9.1 267.0 all-gather.1
where the time goes:
time: 341 us; the launch traced here: 335 us
  waiting for transfers between devices  162 us (48%)
  other arithmetic  67.2 us (20%)
  local copies, waits for them, and re-layouts  46.8 us (14%)
  matrix products  38.3 us (11%)
  between operations  14.1 us (4%)
  starting transfers between devices  6.73 us (2%)
    ppermute x2, waiting for transfers between devices, padded_2(): lax.ppermute(head, axis, [((i + 1) % count, i) for i in range(count)])  161 us
    dot_general x1, matrix products, body(): jnp.einsum('nm,mvkij->nvkij', own_rows, lax.all_gather(state, 'inst', axi...  38.3 us
    sub x3, other arithmetic, direction_residual(): face_flux = central - dissipation * radius_face[..., None, :, :, :] * fourth  33.4 us
    slice x11, local copies, waits for them, and re-layouts, edge_pad(): return jnp.pad(array, pad_widths, mode='edge')  30.6 us
    concatenate x2, other arithmetic, edge_pad(): return jnp.pad(array, pad_widths, mode='edge')  7.23 us
    unnamed x29, local copies, waits for them, and re-layouts  6.95 us
  transfers between devices with their start and end apart: 5, of which 1 were waited for; matrix products, arithmetic and copies ran while one was open for 33% of the time, Pallas kernels for 0%

commit v1 on v0

v1 whole, which is shorter than its diff:
```python
import math

import jax
import jax.numpy as jnp
import numpy as np
from jax import lax
from jax.experimental import pallas as pl
from jax.experimental.pallas import tpu as pltpu
from jax.sharding import PartitionSpec as P

NT = 32
NJ = 128
TILE = 8

dissipation = 0.03125
viscosity = 0.2
frequency = 0.25


def kernel_row(size):
    row = np.zeros(size)
    for k in range(1, size):
        if 2 * k != size:
            row[k] = 0.5 * (-1.0) ** k / math.tan(math.pi * k / size)
    return row


def skew_sums(values, row):
    size = len(values)
    at = lambda n: values[n % size] if (n // size) % 2 == 0 else -values[n % size]
    out = []
    for n in range(size):
        total = None
        for m in range(size):
            k = n - m
            weight = row[k % size] if k >= 0 else -row[k % size]
            if weight == 0.0:
                continue
            term = np.float32(weight) * values[m]
            total = term if total is None else total + term
        out.append(total)
    return out


def circular_sums(values, row):
    size = len(values)
    half = size // 2
    if size == 2:
        return None
    plus = [values[n] + values[n + half] for n in range(half)]
    minus = [values[n] - values[n + half] for n in range(half)]
    even = circular_sums(plus, 0.5 * (row[:half] + row[half:]))
    odd = skew_sums(minus, 0.5 * (row[:half] - row[half:]))
    if even is None:
        return odd + [-value for value in odd]
    return [a + b for a, b in zip(even, odd)] + [a - b for a, b in zip(even, odd)]


def time_kernel(state_ref, out_ref):
    row = frequency * kernel_row(NT)

    def step(tile, carry):
        rows = pl.ds(pl.multiple_of(tile * TILE, TILE), TILE)
        values = [state_ref[n, rows, :] for n in range(NT)]
        for n, value in enumerate(circular_sums(values, row)):
            out_ref[n, rows, :] = value
        return carry

    lax.fori_loop(0, state_ref.shape[1] // TILE, step, 0)


def time_terms(gathered):
    return pl.pallas_call(
        time_kernel,
        out_shape=jax.ShapeDtypeStruct(gathered.shape, jnp.float32),
        in_specs=[pl.BlockSpec(memory_space=pltpu.VMEM)],
        out_specs=pl.BlockSpec(memory_space=pltpu.VMEM),
        compiler_params=pltpu.CompilerParams(vmem_limit_bytes=32 * 2**20),
        cost_estimate=pl.CostEstimate(
            flops=24 * gathered.size, bytes_accessed=8 * gathered.size, transcendentals=0
        ),
    )(gathered)


def primitives(q):
    inverse = 1.0 / q[0]
    speed = [q[1] * inverse, q[2] * inverse, q[3] * inverse]
    pressure = 0.4 * (q[4] - 0.5 * (q[1] * speed[0] + q[2] * speed[1] + q[3] * speed[2]))
    sound = jnp.sqrt(1.4 * pressure * inverse)
    return speed, pressure, sound


def along(speed, sound, normal):
    normal_speed = speed[0] * normal[0] + speed[1] * normal[1] + speed[2] * normal[2]
    area = jnp.sqrt(normal[0] * normal[0] + normal[1] * normal[1] + normal[2] * normal[2])
    return normal_speed, jnp.abs(normal_speed) + sound * area


def flux(v, q, normal_speed, pressure, normal):
    if v in (1, 2, 3):
        return q * normal_speed + pressure * normal[v - 1]
    if v == 4:
        return (q + pressure) * normal_speed
    return q * normal_speed


def spatial_kernel(
    state_ref, halo_ref, metric_ref, metric_halo_ref, volume_ref, time_ref, out_ref, prim_ref, span_ref
):
    depth, height, width = state_ref.shape[2:]
    lane = lax.broadcasted_iota(jnp.int32, (height, width), 1)
    first = lane == 0
    last = lane == width - 1
    back = lambda x: pltpu.roll(x, 1, 1)
    ahead = lambda x: pltpu.roll(x, width - 1, 1)
    rows = height + TILE
    down = lambda x: pltpu.roll(x, 1, 0)
    up = lambda x: pltpu.roll(x, rows - 1, 0)

    def prepare(k, carry):
        q = [state_ref[0, v, k] for v in range(6)]
        speed, pressure, sound = primitives(q)
        for v in range(3):
            prim_ref[v, k] = speed[v]
        prim_ref[3, k] = pressure
        prim_ref[4, k] = sound
        normal = [metric_ref[2, c, k] for c in range(3)]
        normal_speed, radius = along(speed, sound, normal)
        span_ref[6, k] = radius
        for v in range(6):
            span_ref[v, k] = flux(v, q[v], normal_speed, pressure, normal)
        return carry

    lax.fori_loop(0, depth, prepare, 0)

    def step(k, carry):
        speed = [prim_ref[v, k] for v in range(3)]
        pressure = prim_ref[3, k]
        sound = prim_ref[4, k]
        halo = [halo_ref[0, v, k] for v in range(6)]
        halo_speed, halo_pressure, halo_sound = primitives(halo)
        join = lambda a, b: jnp.concatenate([a, b], axis=0)
        wrap_normal = [join(metric_ref[0, c, k], metric_halo_ref[c, k]) for c in range(3)]
        wrap_pressure = join(pressure, halo_pressure)
        wrap_speed, wrap_radius = along(
            [join(a, b) for a, b in zip(speed, halo_speed)], join(sound, halo_sound), wrap_normal
        )
        wrap_weight = dissipation * (wrap_radius + down(wrap_radius))
        wall_normal = [metric_ref[1, c, k] for c in range(3)]
        wall_speed, wall_radius = along(speed, sound, wall_normal)
        wall_weight = dissipation * (wall_radius + jnp.where(first, wall_radius, back(wall_radius)))
        wall_end = (2.0 * dissipation) * wall_radius
        volume = volume_ref[k]
        squared = (
            wall_normal[0] * wall_normal[0] + wall_normal[1] * wall_normal[1] + wall_normal[2] * wall_normal[2]
        )
        coefficient = viscosity * (1.0 + state_ref[0, 5, k]) * (squared / volume)
        coefficient = coefficient + back(coefficient)
        k1 = jnp.maximum(k - 1, 0)
        k2 = jnp.maximum(k - 2, 0)
        k3 = jnp.minimum(k + 1, depth - 1)
        k4 = jnp.minimum(k + 2, depth - 1)
        span_low = dissipation * (span_ref[6, k] + span_ref[6, k1])
        span_high = dissipation * (span_ref[6, k] + span_ref[6, k3])

        for v in range(6):
            q = state_ref[0, v, k]
            cells = join(q, halo[v])
            face = flux(v, cells, wrap_speed, wrap_pressure, wrap_normal)
            step_one = cells - down(cells)
            step_two = up(step_one) - step_one
            step_three = step_two - down(step_two)
            face = face + down(face) - wrap_weight * step_three
            total = (up(face) - face)[:height]
            cell = flux(v, q, wall_speed, pressure, wall_normal)
            step_one = jnp.where(first, 0.0, q - back(q))
            step_two = ahead(step_one) - step_one
            step_three = step_two - jnp.where(first, 0.0, back(step_two))
            face = cell + jnp.where(first, cell, back(cell)) - wall_weight * step_three
            if v > 0:
                face = face - coefficient * step_one
            end = 2.0 * cell - wall_end * step_one
            total = total + (jnp.where(last, end, ahead(face)) - face)
            q1 = state_ref[0, v, k1]
            q2 = state_ref[0, v, k2]
            q3 = state_ref[0, v, k3]
            q4 = state_ref[0, v, k4]
            total = total + (span_ref[v, k3] - span_ref[v, k1])
            total = total - span_high * (q4 - q1 - 3.0 * (q3 - q))
            total = total + span_low * (q3 - q2 - 3.0 * (q - q1))
            term = jnp.concatenate([time_ref[2 * k, 0, v], time_ref[2 * k + 1, 0, v]], axis=0)
            out_ref[0, v, k] = 0.5 * total + volume * term
        return carry

    lax.fori_loop(0, depth, step, 0)


def residual_of(state, halo, metrics, metric_halo, volume, time_term):
    count, variables, depth, height, width = state.shape
    owners = time_term.shape[0]
    whole = lambda a: pl.BlockSpec(a.shape, lambda n: (0,) * a.ndim)
    each = lambda a: pl.BlockSpec((1,) + a.shape[1:], lambda n: (n,) + (0,) * (a.ndim - 1))
    return pl.pallas_call(
        spatial_kernel,
        grid=(count,),
        out_shape=jax.ShapeDtypeStruct(state.shape, jnp.float32),
        in_specs=[
            each(state),
            each(halo),
            whole(metrics),
            whole(metric_halo),
            whole(volume),
            pl.BlockSpec((owners, 1) + time_term.shape[2:], lambda n: (0, n, 0, 0, 0)),
        ],
        out_specs=each(state),
        scratch_shapes=[
            pltpu.VMEM((5, depth, height, width), jnp.float32),
            pltpu.VMEM((7, depth, height, width), jnp.float32),
        ],
        compiler_params=pltpu.CompilerParams(vmem_limit_bytes=48 * 2**20),
        cost_estimate=pl.CostEstimate(
            flops=400 * count * depth * height * width,
            bytes_accessed=12 * state.size + 4 * metrics.size,
            transcendentals=0,
        ),
    )(state, halo, metrics, metric_halo, volume, time_term)


def wrap_halos(state, metrics):
    count = lax.axis_size("wrap")
    onward = [(i, (i + 1) % count) for i in range(count)]
    backward = [((i + 1) % count, i) for i in range(count)]
    inst_count, variables, depth, height, width = state.shape
    pack = lambda cells, face: jnp.concatenate(
        [cells.reshape(-1, width), face.reshape(-1, width)], axis=0
    )
    size = inst_count * variables * depth * 2
    before = lax.ppermute(pack(state[..., -2:, :], metrics[0, :, :, -1:]), "wrap", onward)
    after = lax.ppermute(pack(state[..., :2, :], metrics[0, :, :, :1]), "wrap", backward)
    cells = lambda packed: packed[:size].reshape(inst_count, variables, depth, 2, width)
    face = lambda packed: packed[size:].reshape(3, depth, 1, width)
    halo = jnp.concatenate([cells(after), cells(after), cells(before), cells(before)], axis=-2)
    metric_halo = jnp.concatenate([face(after)] * 4 + [face(before)] * 4, axis=-2)
    return halo, metric_halo


def body(state, metrics, volume):
    inst_count, variables, depth, height, width = state.shape
    owners = lax.axis_size("inst")
    parts = owners // depth
    lines = height // parts
    halo, metric_halo = wrap_halos(state, metrics)
    sent = state.reshape(inst_count, variables, depth, parts, lines, width)
    sent = sent.transpose(2, 3, 0, 1, 4, 5).reshape(owners, inst_count * variables * lines, width)
    held = lax.all_to_all(sent, "inst", 0, 0, tiled=True)
    held = held.reshape(owners * inst_count, variables * lines, width)
    terms = time_terms(held).reshape(owners, inst_count * variables * lines, width)
    terms = lax.all_to_all(terms, "inst", 0, 0, tiled=True)
    terms = terms.reshape(owners, inst_count, variables, lines, width)
    return residual_of(state, halo, metrics, metric_halo, volume, terms)


def solution(mesh):
    in_specs = (
        P("inst", None, None, "wrap", None),
        P(None, None, None, "wrap", None),
        P(None, "wrap", None),
    )
    out_specs = P("inst", None, None, "wrap", None)
    return jax.shard_map(body, mesh=mesh, in_specs=in_specs, out_specs=out_specs, check_vma=False)
```

time: 341 us -> 105 us (0.31)
  the two profiles are of different devices: /device:TPU:225 before, /device:TPU:6 now
where the time goes in v1:
time: 105 us
  blocking collectives  47.5 us (45%)
  waiting for transfers between devices  30.9 us (29%)
  Pallas kernels  10.4 us (10%)
  starting transfers between devices  8.97 us (9%)
  local copies, waits for them, and re-layouts  6.51 us (6%)
    all_to_all x1, blocking collectives, body(): held = lax.all_to_all(sent, 'inst', 0, 0, tiled=True)  47.5 us
    all_to_all x1, waiting for transfers between devices, body(): terms = lax.all_to_all(terms, 'inst', 0, 0, tiled=True)  28.3 us
    pallas_call x1, Pallas kernels, residual_of(): pl.pallas_call(spatial_kernel, grid=(count,), out_shape=jax.ShapeDtypeStr...  7.88 us
    all_to_all x1, starting transfers between devices, body(): terms = lax.all_to_all(terms, 'inst', 0, 0, tiled=True)  4.68 us
    ppermute x1, starting transfers between devices, wrap_halos(): lax.ppermute(pack(state[..., :2, :], metrics[0, :, :, :1]), 'wrap', backw...  4.21 us
    unnamed x8, local copies, waits for them, and re-layouts  3.07 us
    ppermute x1, waiting for transfers between devices, wrap_halos(): lax.ppermute(pack(state[..., -2:, :], metrics[0, :, :, -1:]), 'wrap', onw...  2.59 us
    pallas_call x1, Pallas kernels, time_terms(): pl.pallas_call(time_kernel, out_shape=jax.ShapeDtypeStruct(gathered.shape...  2.53 us
  transfers between devices with their start and end apart: 3, of which 2 were waited for; matrix products, arithmetic and copies ran while one was open for 2% of the time, Pallas kernels for 0%

profile of v1, /device:TPU:6, one launch (start us, length us, event | category | flops | bytes accessed | tf_op | source)
XLA Modules:
  0.0 104.6 jit_solution(5841627771572911942)
XLA Ops:
  0.0 1.6 %copy.4 = f32[8,2,2,6,16,128]{5,4,3,2,1,0:T(8,128)S(1)} copy(f32[8,2,2,6,16,128]{5,4,1,0,3,2:T(8,128)} %bitcast.15) | data formatting | bytes 3145728 | tf_op jit(solution)/shard_map/transpose | solution.py:254
  1.6 47.5 %all_to_all.10 = f32[16,192,128]{2,1,0:T(8,128)S(1)} all-to-all(f32[16,192,128]{2,1,0:T(8,128)S(1)} %bitcast.18), channel_id=1, replica_groups=mesh['wrap'=16,'inst'=16] {'inst'}, dimensions={0} | all-to-all | bytes 3145728 | tf_op jit(solution)/shard_map/all_to_all | solution.py:255
  49.2 2.5 %shard_map.37 = f32[32,96,128]{2,1,0:T(8,128)} custom-call(f32[32,96,128]{2,1,0:T(8,128)S(1)} %bitcast.16), custom_call_target="tpu_custom_call" | custom-call | flops 9437184 | bytes 3145728 | tf_op jit(solution)/shard_map/pallas_call | solution.py:73
  51.7 0.0 copy-start
  51.7 4.7 %all-to-all-start.1 = ((f32[16,192,128]{2,1,0:T(8,128)}), f32[16,192,128]{2,1,0:T(8,128)S(1)}, u32[]{:S(2)}, u32[]{:S(2)}) async-start(f32[16,192,128]{2,1,0:T(8,128)} %bitcast.12), calls=%async_computation.1 | async-start | bytes 3145728 | tf_op jit(solution)/shard_map/all_to_all | solution.py:258
  56.4 1.0 fusion.1
  57.4 0.0 copy-done
  57.4 0.1 fusion
  57.5 0.1 collective-permute-start.1
  57.6 4.2 %collective-permute-start = (f32[216,128]{1,0:T(8,128)S(1)}, f32[216,128]{1,0:T(8,128)S(1)}, u32[]{:S(2)}, u32[]{:S(2)}) collective-permute-start(f32[216,128]{1,0:T(8,128)S(1)} %pad_maximum_fusion.1), channel_id=1, source_target_pairs={{16,0},{32,16},{48,32},{64,48},{80,64},{96,80},{112,96},{128,112},... | collective-permute-start | bytes 331784 | tf_op jit(solution)/shard_map/ppermute | solution.py:239
  61.8 2.6 %collective-permute-done.1 = f32[216,128]{1,0:T(8,128)S(1)} collective-permute-done((f32[216,128]{1,0:T(8,128)S(1)}, f32[216,128]{1,0:T(8,128)S(1)}, u32[]{:S(2)}, u32[]{:S(2)}) %collective-permute-start.1) | collective-permute-done | bytes 110624 | tf_op jit(solution)/shard_map/ppermute | solution.py:238
  64.4 0.0 collective-permute-done
  64.4 0.8 concatenate.15.metric_halo_ref
  65.2 0.2 pad_maximum_fusion.halo_ref
  65.3 28.3 %all-to-all-done.1 = f32[16,192,128]{2,1,0:T(8,128)S(1)} async-done(((f32[16,192,128]{2,1,0:T(8,128)}), f32[16,192,128]{2,1,0:T(8,128)S(1)}, u32[]{:S(2)}, u32[]{:S(2)}) %all-to-all-start.1) | async-done | bytes 1572896 | tf_op jit(solution)/shard_map/all_to_all | solution.py:258
  93.6 0.0 copy-start.1
  93.6 1.3 %copy-done.1 = f32[3,3,8,32,128]{4,3,2,1,0:T(8,128)S(1)} copy-done((f32[3,3,8,32,128]{4,3,2,1,0:T(8,128)S(1)}, f32[3,3,8,32,128]{4,3,2,1,0:T(8,128)}, u32[]{:S(2)}) %copy-start.1) | copy-done | bytes 1179672
  94.9 0.0 copy-start.2
  94.9 0.9 copy-done.2
  95.8 0.0 copy-start.3
  95.8 0.9 copy-done.3
  96.7 7.9 %shard_map.38 = f32[2,6,8,32,128]{4,3,2,1,0:T(8,128)} custom-call(f32[2,6,8,32,128]{4,3,2,1,0:T(8,128)S(1)} %copy-done, f32[2,6,8,8,128]{4,3,2,1,0:T(8,128)S(1)} %pad_maximum_fusion.halo_ref, f32[3,3,8,32,128]{4,3,2,1,0:T(8,128)S(1)} %copy-done.1, f32[3,8,8,128]{3,2,1,0:T(8,128)S(1)} %copy-done.2, f32[8,32,128]{2,1,0:T(8,128)S(1)} %copy-done.3, ...), custom_call_target="tpu_custom_call" | custom-call | flops 26214400 | bytes 5898240 | tf_op jit(solution)/shard_map/pallas_call | solution.py:203
  (6 shorter events, 0.0 us)
Async XLA Ops:
  51.7 5.7 %copy-start = (f32[2,6,8,32,128]{4,3,2,1,0:T(8,128)S(1)}, f32[2,6,8,32,128]{4,3,2,1,0:T(8,128)}, u32[]{:S(2)}) copy-start(f32[2,6,8,32,128]{4,3,2,1,0:T(8,128)} %state_ref.1) | copy-start | bytes 4718596
  51.7 41.9 %all-to-all-start.1 = ((f32[16,192,128]{2,1,0:T(8,128)}), f32[16,192,128]{2,1,0:T(8,128)S(1)}, u32[]{:S(2)}, u32[]{:S(2)}) async-start(f32[16,192,128]{2,1,0:T(8,128)} %bitcast.12), calls=%async_computation.1 | async-start | bytes 3145728 | tf_op jit(solution)/shard_map/all_to_all | solution.py:258
  57.5 6.9 %collective-permute-start.1 = (f32[216,128]{1,0:T(8,128)S(1)}, f32[216,128]{1,0:T(8,128)S(1)}, u32[]{:S(2)}, u32[]{:S(2)}) collective-permute-start(f32[216,128]{1,0:T(8,128)S(1)} %pad_maximum_fusion.2), channel_id=1, source_target_pairs={{0,16},{16,32},{32,48},{48,64},{64,80},{80,96},{96,112},{112,128},... | collective-permute-start | bytes 331784 | tf_op jit(solution)/shard_map/ppermute | solution.py:238
  57.6 6.8 %collective-permute-start = (f32[216,128]{1,0:T(8,128)S(1)}, f32[216,128]{1,0:T(8,128)S(1)}, u32[]{:S(2)}, u32[]{:S(2)}) collective-permute-start(f32[216,128]{1,0:T(8,128)S(1)} %pad_maximum_fusion.1), channel_id=1, source_target_pairs={{16,0},{32,16},{48,32},{64,48},{80,64},{96,80},{112,96},{128,112},... | collective-permute-start | bytes 331784 | tf_op jit(solution)/shard_map/ppermute | solution.py:239
  93.6 1.3 %copy-start.1 = (f32[3,3,8,32,128]{4,3,2,1,0:T(8,128)S(1)}, f32[3,3,8,32,128]{4,3,2,1,0:T(8,128)}, u32[]{:S(2)}) copy-start(f32[3,3,8,32,128]{4,3,2,1,0:T(8,128)} %metric_ref.1) | copy-start | bytes 3538948
  94.9 0.9 copy-start.2
  95.8 0.9 copy-start.3

commit v2 on v1

--- a/solution.py
+++ b/solution.py
@@ -1,3 +1,4 @@
+import functools
 import math
 
 import jax
@@ -15,6 +16,7 @@
 dissipation = 0.03125
 viscosity = 0.2
 frequency = 0.25
+GROUPS = (6,)
 
 
 def kernel_row(size):
@@ -105,7 +107,7 @@
 
 
 def spatial_kernel(
-    state_ref, halo_ref, metric_ref, metric_halo_ref, volume_ref, time_ref, out_ref, prim_ref, span_ref
+    state_ref, halo_ref, metric_ref, metric_halo_ref, volume_ref, out_ref, prim_ref, span_ref
 ):
     depth, height, width = state_ref.shape[2:]
     lane = lax.broadcasted_iota(jnp.int32, (height, width), 1)
@@ -188,16 +190,14 @@
             total = total + (span_ref[v, k3] - span_ref[v, k1])
             total = total - span_high * (q4 - q1 - 3.0 * (q3 - q))
             total = total + span_low * (q3 - q2 - 3.0 * (q - q1))
-            term = jnp.concatenate([time_ref[2 * k, 0, v], time_ref[2 * k + 1, 0, v]], axis=0)
-            out_ref[0, v, k] = 0.5 * total + volume * term
+            out_ref[0, v, k] = 0.5 * total
         return carry
 
     lax.fori_loop(0, depth, step, 0)
 
 
-def residual_of(state, halo, metrics, metric_halo, volume, time_term):
+def spatial(state, halo, metrics, metric_halo, volume):
     count, variables, depth, height, width = state.shape
-    owners = time_term.shape[0]
     whole = lambda a: pl.BlockSpec(a.shape, lambda n: (0,) * a.ndim)
     each = lambda a: pl.BlockSpec((1,) + a.shape[1:], lambda n: (n,) + (0,) * (a.ndim - 1))
     return pl.pallas_call(
@@ -210,7 +210,6 @@
             whole(metrics),
             whole(metric_halo),
             whole(volume),
-            pl.BlockSpec((owners, 1) + time_term.shape[2:], lambda n: (0, n, 0, 0, 0)),
         ],
         out_specs=each(state),
         scratch_shapes=[
@@ -223,7 +222,42 @@
             bytes_accessed=12 * state.size + 4 * metrics.size,
             transcendentals=0,
         ),
-    )(state, halo, metrics, metric_halo, volume, time_term)
+    )(state, halo, metrics, metric_halo, volume)
+
+
+def combine_kernel(groups, spatial_ref, volume_ref, *refs):
+    out_ref = refs[-1]
+    depth = spatial_ref.shape[2]
+    parts = refs[0].shape[0] // depth
+
+    def step(k, carry):
+        volume = volume_ref[k]
+        v = 0
+        for ref, count in zip(refs, groups):
+            for w in range(count):
+                term = jnp.concatenate([ref[parts * k + p, 0, w] for p in range(parts)], axis=0)
+                out_ref[0, v, k] = spatial_ref[0, v, k] + volume * term
+                v += 1
+        return carry
+
+    lax.fori_loop(0, depth, step, 0)
+
+
+def combined(local, volume, terms):
+    whole = lambda a: pl.BlockSpec(a.shape, lambda n: (0,) * a.ndim)
+    each = lambda a: pl.BlockSpec((1,) + a.shape[1:], lambda n: (n,) + (0,) * (a.ndim - 1))
+    owned = lambda a: pl.BlockSpec((a.shape[0], 1) + a.shape[2:], lambda n: (0, n, 0, 0, 0))
+    return pl.pallas_call(
+        functools.partial(combine_kernel, [term.shape[2] for term in terms]),
+        grid=(local.shape[0],),
+        out_shape=jax.ShapeDtypeStruct(local.shape, jnp.float32),
+        in_specs=[each(local), whole(volume)] + [owned(term) for term in terms],
+        out_specs=each(local),
+        compiler_params=pltpu.CompilerParams(vmem_limit_bytes=32 * 2**20),
+        cost_estimate=pl.CostEstimate(
+            flops=2 * local.size, bytes_accessed=12 * local.size, transcendentals=0
+        ),
+    )(local, volume, *terms)
 
 
 def wrap_halos(state, metrics):
@@ -250,14 +284,22 @@
     parts = owners // depth
     lines = height // parts
     halo, metric_halo = wrap_halos(state, metrics)
-    sent = state.reshape(inst_count, variables, depth, parts, lines, width)
-    sent = sent.transpose(2, 3, 0, 1, 4, 5).reshape(owners, inst_count * variables * lines, width)
-    held = lax.all_to_all(sent, "inst", 0, 0, tiled=True)
-    held = held.reshape(owners * inst_count, variables * lines, width)
-    terms = time_terms(held).reshape(owners, inst_count * variables * lines, width)
-    terms = lax.all_to_all(terms, "inst", 0, 0, tiled=True)
-    terms = terms.reshape(owners, inst_count, variables, lines, width)
-    return residual_of(state, halo, metrics, metric_halo, volume, terms)
+    split = state.reshape(inst_count, variables, depth, parts, lines, width)
+    held = []
+    first = 0
+    for count in GROUPS:
+        sent = split[:, first : first + count].transpose(2, 3, 0, 1, 4, 5)
+        sent = sent.reshape(owners, inst_count * count * lines, width)
+        held.append(lax.all_to_all(sent, "inst", 0, 0, tiled=True))
+        first += count
+    local = spatial(state, halo, metrics, metric_halo, volume)
+    terms = []
+    for part, count in zip(held, GROUPS):
+        part = time_terms(part.reshape(owners * inst_count, count * lines, width))
+        part = part.reshape(owners, inst_count * count * lines, width)
+        part = lax.all_to_all(part, "inst", 0, 0, tiled=True)
+        terms.append(part.reshape(owners, inst_count, count, lines, width))
+    return combined(local, volume, terms)
 
 
 def solution(mesh):

time: 105 us -> 96.7 us (0.921)
  waiting for transfers between devices: 30.9 us -> 20.8 us
  local copies, waits for them, and re-layouts: 6.51 us -> 8.19 us
    all_to_all x1, waiting for transfers between devices: 28.3 us -> 18.2 us  [body(): part = lax.all_to_all(part, 'inst', 0, 0, tiled=True)]
    unnamed x8 -> x12, local copies, waits for them, and re-layouts: 3.07 us -> 4.45 us
    pallas_call x1 -> x2, Pallas kernels: 7.88 us -> 8.06 us  [the longest x1 6.69 us: spatial(): pl.pallas_call(spatial_kernel, grid=(count,), out_shape=jax.ShapeDtypeStr...]
  transfers between devices with their start and end apart: 3 -> 3, of which waited for: 2 -> 2; matrix products, arithmetic and copies ran while one was open for 2% -> 2% of each run, Pallas kernels for 0% -> 7%
where the time goes in v2:
time: 96.7 us; the launch traced here: 96.4 us
  blocking collectives  47.5 us (49%)
  waiting for transfers between devices  20.8 us (22%)
  Pallas kernels  10.6 us (11%)
  starting transfers between devices  8.97 us (9%)
  local copies, waits for them, and re-layouts  8.19 us (8%)
    all_to_all x1, blocking collectives, body(): held.append(lax.all_to_all(sent, 'inst', 0, 0, tiled=True))  47.5 us
    all_to_all x1, waiting for transfers between devices, body(): part = lax.all_to_all(part, 'inst', 0, 0, tiled=True)  18.2 us
    pallas_call x1, Pallas kernels, spatial(): pl.pallas_call(spatial_kernel, grid=(count,), out_shape=jax.ShapeDtypeStr...  6.69 us
    all_to_all x1, starting transfers between devices, body(): part = lax.all_to_all(part, 'inst', 0, 0, tiled=True)  4.68 us
    unnamed x12, local copies, waits for them, and re-layouts  4.45 us
    ppermute x1, starting transfers between devices, wrap_halos(): lax.ppermute(pack(state[..., :2, :], metrics[0, :, :, :1]), 'wrap', backw...  4.21 us
    ppermute x1, waiting for transfers between devices, wrap_halos(): lax.ppermute(pack(state[..., -2:, :], metrics[0, :, :, -1:]), 'wrap', onw...  2.58 us
    pallas_call x1, Pallas kernels, time_terms(): pl.pallas_call(time_kernel, out_shape=jax.ShapeDtypeStruct(gathered.shape...  2.54 us
  transfers between devices with their start and end apart: 3, of which 2 were waited for; matrix products, arithmetic and copies ran while one was open for 2% of the time, Pallas kernels for 7%

profile of v2, /device:TPU:6, one launch (start us, length us, event | category | flops | bytes accessed | tf_op | source)
XLA Modules:
  0.0 96.4 jit_solution(6213762737914796010)
XLA Ops:
  0.0 1.6 %copy.4 = f32[8,2,2,6,16,128]{5,4,3,2,1,0:T(8,128)S(1)} copy(f32[8,2,2,6,16,128]{5,4,1,0,3,2:T(8,128)} %bitcast.15) | data formatting | bytes 3145728 | tf_op jit(solution)/shard_map/transpose | solution.py:291
  1.6 47.5 %all_to_all.10 = f32[16,192,128]{2,1,0:T(8,128)S(1)} all-to-all(f32[16,192,128]{2,1,0:T(8,128)S(1)} %bitcast.18), channel_id=1, replica_groups=mesh['wrap'=16,'inst'=16] {'inst'}, dimensions={0} | all-to-all | bytes 3145728 | tf_op jit(solution)/shard_map/all_to_all | solution.py:293
  49.2 2.5 %shard_map.38 = f32[32,96,128]{2,1,0:T(8,128)} custom-call(f32[32,96,128]{2,1,0:T(8,128)S(1)} %bitcast.16), custom_call_target="tpu_custom_call" | custom-call | flops 9437184 | bytes 3145728 | tf_op jit(solution)/shard_map/pallas_call | solution.py:75
  51.7 4.7 %all-to-all-start.1 = ((f32[16,192,128]{2,1,0:T(8,128)}), f32[16,192,128]{2,1,0:T(8,128)S(1)}, u32[]{:S(2)}, u32[]{:S(2)}) async-start(f32[16,192,128]{2,1,0:T(8,128)} %bitcast.12), calls=%async_computation.1 | async-start | bytes 3145728 | tf_op jit(solution)/shard_map/all_to_all | solution.py:300
  56.4 0.0 copy-start.4
  56.4 1.0 %fusion.1 = (f32[1,3,8,1,128]{4,3,2,1,0:T(1,128)S(1)}, f32[1,3,8,1,128]{4,3,2,1,0:T(1,128)S(1)}) fusion(f32[3,3,8,32,128]{4,3,2,1,0:T(8,128)} %metric_ref.1), kind=kLoop, calls=%fused_computation.4 | loop fusion | bytes 49152 | tf_op jit(solution)/shard_map/slice | solution.py:273
  57.4 0.0 copy-done
  57.4 0.1 fusion
  57.5 0.1 collective-permute-start.1
  57.6 4.2 %collective-permute-start = (f32[216,128]{1,0:T(8,128)S(1)}, f32[216,128]{1,0:T(8,128)S(1)}, u32[]{:S(2)}, u32[]{:S(2)}) collective-permute-start(f32[216,128]{1,0:T(8,128)S(1)} %pad_maximum_fusion.1), channel_id=1, source_target_pairs={{16,0},{32,16},{48,32},{64,48},{80,64},{96,80},{112,96},{128,112},... | collective-permute-start | bytes 331784 | tf_op jit(solution)/shard_map/ppermute | solution.py:273
  61.8 2.6 %collective-permute-done.1 = f32[216,128]{1,0:T(8,128)S(1)} collective-permute-done((f32[216,128]{1,0:T(8,128)S(1)}, f32[216,128]{1,0:T(8,128)S(1)}, u32[]{:S(2)}, u32[]{:S(2)}) %collective-permute-start.1) | collective-permute-done | bytes 110624 | tf_op jit(solution)/shard_map/ppermute | solution.py:272
  64.4 0.0 collective-permute-done
  64.4 0.6 copy-done.5
  65.1 0.1 concatenate.15.metric_halo_ref
  65.2 0.9 slice.34
  66.1 0.2 pad_maximum_fusion.halo_ref
  66.3 0.0 copy-start.3
  66.3 1.3 %copy-done.3 = f32[3,3,8,32,128]{4,3,2,1,0:T(8,128)S(1)} copy-done((f32[3,3,8,32,128]{4,3,2,1,0:T(8,128)S(1)}, f32[3,3,8,32,128]{4,3,2,1,0:T(8,128)}, u32[]{:S(2)}) %copy-start.3) | copy-done | bytes 1179672
  67.6 6.7 %shard_map.37.spatial_ref = f32[2,6,8,32,128]{4,3,2,1,0:T(8,128)S(1)} custom-call(f32[2,6,8,32,128]{4,3,2,1,0:T(8,128)S(1)} %copy-done, f32[2,6,8,8,128]{4,3,2,1,0:T(8,128)S(1)} %pad_maximum_fusion.halo_ref, f32[3,3,8,32,128]{4,3,2,1,0:T(8,128)S(1)} %copy-done.3, f32[3,8,8,128]{3,2,1,0:T(8,128)S(1)} %concatenate.15.metric_halo_ref, f32[8,32,128]{2,1,0:T(8,128)S(1)} %copy-done.4), custom_call_target="tpu_custom_call" | custom-call | flops 26214400 | bytes 5898240 | tf_op jit(solution)/shard_map/pallas_call | solution.py:203
  74.3 0.0 copy-start.1
  74.3 1.1 %copy-done.1 = f32[2,6,8,32,128]{4,3,2,1,0:T(8,128)} copy-done((f32[2,6,8,32,128]{4,3,2,1,0:T(8,128)}, f32[2,6,8,32,128]{4,3,2,1,0:T(8,128)S(1)}, u32[]{:S(2)}) %copy-start.1) | copy-done | bytes 1572888
  75.4 18.2 %all-to-all-done.1 = f32[16,192,128]{2,1,0:T(8,128)S(1)} async-done(((f32[16,192,128]{2,1,0:T(8,128)}), f32[16,192,128]{2,1,0:T(8,128)S(1)}, u32[]{:S(2)}, u32[]{:S(2)}) %all-to-all-start.1) | async-done | bytes 1572896 | tf_op jit(solution)/shard_map/all_to_all | solution.py:300
  93.6 1.4 %copy-done.2 = f32[2,6,8,32,128]{4,3,2,1,0:T(8,128)S(1)} copy-done((f32[2,6,8,32,128]{4,3,2,1,0:T(8,128)S(1)}, f32[2,6,8,32,128]{4,3,2,1,0:T(8,128)}, u32[]{:S(2)}) %copy-start.2) | copy-done | bytes 1572888
  95.0 1.4 %shard_map.39 = f32[2,6,8,32,128]{4,3,2,1,0:T(8,128)} custom-call(f32[2,6,8,32,128]{4,3,2,1,0:T(8,128)S(1)} %copy-done.2, f32[8,32,128]{2,1,0:T(8,128)S(1)} %copy-done.4, f32[16,2,6,16,128]{4,3,2,1,0:T(8,128)S(1)} %bitcast.17), custom_call_target="tpu_custom_call" | custom-call | flops 786432 | bytes 4718592 | tf_op jit(solution)/shard_map/pallas_call | solution.py:250
  (9 shorter events, 0.0 us)
Async XLA Ops:
  51.7 5.7 %copy-start = (f32[2,6,8,32,128]{4,3,2,1,0:T(8,128)S(1)}, f32[2,6,8,32,128]{4,3,2,1,0:T(8,128)}, u32[]{:S(2)}) copy-start(f32[2,6,8,32,128]{4,3,2,1,0:T(8,128)} %state_ref.1) | copy-start | bytes 4718596
  51.7 41.9 %all-to-all-start.1 = ((f32[16,192,128]{2,1,0:T(8,128)}), f32[16,192,128]{2,1,0:T(8,128)S(1)}, u32[]{:S(2)}, u32[]{:S(2)}) async-start(f32[16,192,128]{2,1,0:T(8,128)} %bitcast.12), calls=%async_computation.1 | async-start | bytes 3145728 | tf_op jit(solution)/shard_map/all_to_all | solution.py:300
  56.4 9.9 %copy-start.4 = (f32[8,32,128]{2,1,0:T(8,128)S(1)}, f32[8,32,128]{2,1,0:T(8,128)}, u32[]{:S(2)}) copy-start(f32[8,32,128]{2,1,0:T(8,128)} %volume_ref.3) | copy-start | bytes 393220
  57.5 6.9 %collective-permute-start.1 = (f32[216,128]{1,0:T(8,128)S(1)}, f32[216,128]{1,0:T(8,128)S(1)}, u32[]{:S(2)}, u32[]{:S(2)}) collective-permute-start(f32[216,128]{1,0:T(8,128)S(1)} %pad_maximum_fusion.2), channel_id=1, source_target_pairs={{0,16},{16,32},{32,48},{48,64},{64,80},{80,96},{96,112},{112,128},... | collective-permute-start | bytes 331784 | tf_op jit(solution)/shard_map/ppermute | solution.py:272
  57.6 6.8 %collective-permute-start = (f32[216,128]{1,0:T(8,128)S(1)}, f32[216,128]{1,0:T(8,128)S(1)}, u32[]{:S(2)}, u32[]{:S(2)}) collective-permute-start(f32[216,128]{1,0:T(8,128)S(1)} %pad_maximum_fusion.1), channel_id=1, source_target_pairs={{16,0},{32,16},{48,32},{64,48},{80,64},{96,80},{112,96},{128,112},... | collective-permute-start | bytes 331784 | tf_op jit(solution)/shard_map/ppermute | solution.py:273
  64.4 0.6 copy-start.5
  66.3 1.3 %copy-start.3 = (f32[3,3,8,32,128]{4,3,2,1,0:T(8,128)S(1)}, f32[3,3,8,32,128]{4,3,2,1,0:T(8,128)}, u32[]{:S(2)}) copy-start(f32[3,3,8,32,128]{4,3,2,1,0:T(8,128)} %metric_ref.1) | copy-start | bytes 3538948
  74.3 1.1 %copy-start.1 = (f32[2,6,8,32,128]{4,3,2,1,0:T(8,128)}, f32[2,6,8,32,128]{4,3,2,1,0:T(8,128)S(1)}, u32[]{:S(2)}) copy-start(f32[2,6,8,32,128]{4,3,2,1,0:T(8,128)S(1)} %shard_map.37.spatial_ref) | copy-start | bytes 4718596
  93.6 1.4 %copy-start.2 = (f32[2,6,8,32,128]{4,3,2,1,0:T(8,128)S(1)}, f32[2,6,8,32,128]{4,3,2,1,0:T(8,128)}, u32[]{:S(2)}) copy-start(f32[2,6,8,32,128]{4,3,2,1,0:T(8,128)} %copy-done.1) | copy-start | bytes 4718596

commit v3 on v1

--- a/solution.py
+++ b/solution.py
@@ -11,6 +11,7 @@
 NT = 32
 NJ = 128
 TILE = 8
+BLOCKS = 2
 
 dissipation = 0.03125
 viscosity = 0.2
@@ -25,21 +26,37 @@
     return row
 
 
+def weighted(pairs):
+    total = None
+    for weight, value in pairs:
+        if abs(weight) > 1e-12:
+            term = np.float32(weight) * value
+            total = term if total is None else total + term
+    return total
+
+
 def skew_sums(values, row):
     size = len(values)
-    at = lambda n: values[n % size] if (n // size) % 2 == 0 else -values[n % size]
-    out = []
-    for n in range(size):
-        total = None
-        for m in range(size):
-            k = n - m
-            weight = row[k % size] if k >= 0 else -row[k % size]
-            if weight == 0.0:
-                continue
-            term = np.float32(weight) * values[m]
-            total = term if total is None else total + term
-        out.append(total)
-    return out
+    half = size // 2
+    if size == 2:
+        return [-np.float32(row[1]) * values[1], np.float32(row[1]) * values[0]]
+    at = lambda k: row[k % size] * (1.0 if (k // size) % 2 == 0 else -1.0)
+    even = [values[0]] + [values[m] - values[size - m] for m in range(1, half)]
+    odd = [None] + [values[m] + values[size - m] for m in range(1, half)] + [values[half]]
+    from_even = [None] + [
+        weighted(
+            [(at(n), even[0])] + [(0.5 * (at(n - m) + at(n + m)), even[m]) for m in range(1, half)]
+        )
+        for n in range(1, half + 1)
+    ]
+    from_odd = [
+        weighted(
+            [(0.5 * (at(n - m) - at(n + m)), odd[m]) for m in range(1, half)] + [(at(n - half), odd[half])]
+        )
+        for n in range(half)
+    ]
+    out = [from_odd[0]] + [from_odd[n] + from_even[n] for n in range(1, half)] + [from_even[half]]
+    return out + [from_even[n] - from_odd[n] for n in range(half - 1, 0, -1)]
 
 
 def circular_sums(values, row):
@@ -75,9 +92,9 @@
         out_shape=jax.ShapeDtypeStruct(gathered.shape, jnp.float32),
         in_specs=[pl.BlockSpec(memory_space=pltpu.VMEM)],
         out_specs=pl.BlockSpec(memory_space=pltpu.VMEM),
-        compiler_params=pltpu.CompilerParams(vmem_limit_bytes=32 * 2**20),
+        compiler_params=pltpu.CompilerParams(vmem_limit_bytes=16 * 2**20),
         cost_estimate=pl.CostEstimate(
-            flops=24 * gathered.size, bytes_accessed=8 * gathered.size, transcendentals=0
+            flops=16 * gathered.size, bytes_accessed=8 * gathered.size, transcendentals=0
         ),
     )(gathered)
 
@@ -105,7 +122,7 @@
 
 
 def spatial_kernel(
-    state_ref, halo_ref, metric_ref, metric_halo_ref, volume_ref, time_ref, out_ref, prim_ref, span_ref
+    state_ref, halo_ref, metric_ref, metric_halo_ref, volume_ref, out_ref, prim_ref, span_ref
 ):
     depth, height, width = state_ref.shape[2:]
     lane = lax.broadcasted_iota(jnp.int32, (height, width), 1)
@@ -188,16 +205,14 @@
             total = total + (span_ref[v, k3] - span_ref[v, k1])
             total = total - span_high * (q4 - q1 - 3.0 * (q3 - q))
             total = total + span_low * (q3 - q2 - 3.0 * (q - q1))
-            term = jnp.concatenate([time_ref[2 * k, 0, v], time_ref[2 * k + 1, 0, v]], axis=0)
-            out_ref[0, v, k] = 0.5 * total + volume * term
+            out_ref[0, v, k] = 0.5 * total
         return carry
 
     lax.fori_loop(0, depth, step, 0)
 
 
-def residual_of(state, halo, metrics, metric_halo, volume, time_term):
+def spatial(state, halo, metrics, metric_halo, volume):
     count, variables, depth, height, width = state.shape
-    owners = time_term.shape[0]
     whole = lambda a: pl.BlockSpec(a.shape, lambda n: (0,) * a.ndim)
     each = lambda a: pl.BlockSpec((1,) + a.shape[1:], lambda n: (n,) + (0,) * (a.ndim - 1))
     return pl.pallas_call(
@@ -210,20 +225,72 @@
             whole(metrics),
             whole(metric_halo),
             whole(volume),
-            pl.BlockSpec((owners, 1) + time_term.shape[2:], lambda n: (0, n, 0, 0, 0)),
         ],
         out_specs=each(state),
         scratch_shapes=[
             pltpu.VMEM((5, depth, height, width), jnp.float32),
             pltpu.VMEM((7, depth, height, width), jnp.float32),
         ],
-        compiler_params=pltpu.CompilerParams(vmem_limit_bytes=48 * 2**20),
+        compiler_params=pltpu.CompilerParams(vmem_limit_bytes=16 * 2**20),
         cost_estimate=pl.CostEstimate(
             flops=400 * count * depth * height * width,
             bytes_accessed=12 * state.size + 4 * metrics.size,
             transcendentals=0,
         ),
-    )(state, halo, metrics, metric_halo, volume, time_term)
+    )(state, halo, metrics, metric_halo, volume)
+
+
+def combine_kernel(spatial_ref, volume_ref, term_ref, out_ref, held_ref, in_sems, out_sems):
+    count, variables, depth = spatial_ref.shape[:3]
+    parts = term_ref.shape[0] // depth
+    run = variables // BLOCKS
+    blocks = [(n, slice(b * run, (b + 1) * run)) for n in range(count) for b in range(BLOCKS)]
+    fetches = [
+        pltpu.make_async_copy(spatial_ref.at[n, r], held_ref.at[n, r], in_sems.at[b])
+        for b, (n, r) in enumerate(blocks)
+    ]
+    writes = [
+        pltpu.make_async_copy(held_ref.at[n, r], out_ref.at[n, r], out_sems.at[b])
+        for b, (n, r) in enumerate(blocks)
+    ]
+    for fetch in fetches:
+        fetch.start()
+    for b, (n, r) in enumerate(blocks):
+        fetches[b].wait()
+
+        def step(k, carry):
+            volume = volume_ref[k]
+            for v in range(r.start, r.stop):
+                term = jnp.concatenate([term_ref[parts * k + p, n, v] for p in range(parts)], axis=0)
+                held_ref[n, v, k] = held_ref[n, v, k] + volume * term
+            return carry
+
+        lax.fori_loop(0, depth, step, 0)
+        writes[b].start()
+    for write in writes:
+        write.wait()
+
+
+def combined(local, volume, terms):
+    count = local.shape[0] * BLOCKS
+    vmem = pl.BlockSpec(memory_space=pltpu.VMEM)
+    anywhere = pl.BlockSpec(memory_space=pl.ANY)
+    return pl.pallas_call(
+        combine_kernel,
+        out_shape=jax.ShapeDtypeStruct(local.shape, jnp.float32),
+        in_specs=[anywhere, vmem, vmem],
+        out_specs=anywhere,
+        input_output_aliases={0: 0},
+        scratch_shapes=[
+            pltpu.VMEM(local.shape, jnp.float32),
+            pltpu.SemaphoreType.DMA((count,)),
+            pltpu.SemaphoreType.DMA((count,)),
+        ],
+        compiler_params=pltpu.CompilerParams(vmem_limit_bytes=16 * 2**20),
+        cost_estimate=pl.CostEstimate(
+            flops=2 * local.size, bytes_accessed=12 * local.size, transcendentals=0
+        ),
+    )(local, volume, terms)
 
 
 def wrap_halos(state, metrics):
@@ -250,14 +317,14 @@
     parts = owners // depth
     lines = height // parts
     halo, metric_halo = wrap_halos(state, metrics)
-    sent = state.reshape(inst_count, variables, depth, parts, lines, width)
-    sent = sent.transpose(2, 3, 0, 1, 4, 5).reshape(owners, inst_count * variables * lines, width)
+    split = state.reshape(inst_count, variables, depth, parts, lines, width)
+    sent = split.transpose(2, 3, 0, 1, 4, 5).reshape(owners, inst_count * variables * lines, width)
     held = lax.all_to_all(sent, "inst", 0, 0, tiled=True)
-    held = held.reshape(owners * inst_count, variables * lines, width)
-    terms = time_terms(held).reshape(owners, inst_count * variables * lines, width)
-    terms = lax.all_to_all(terms, "inst", 0, 0, tiled=True)
+    terms = time_terms(held.reshape(owners * inst_count, variables * lines, width))
+    terms = lax.all_to_all(terms.reshape(sent.shape), "inst", 0, 0, tiled=True)
     terms = terms.reshape(owners, inst_count, variables, lines, width)
-    return residual_of(state, halo, metrics, metric_halo, volume, terms)
+    local = spatial(state, halo, metrics, metric_halo, volume)
+    return combined(local, volume, terms)
 
 
 def solution(mesh):

time: 105 us -> 95.8 us (0.912)
  waiting for transfers between devices: 30.9 us -> 21.1 us
  Pallas kernels: 10.4 us -> 12 us
    all_to_all x1, waiting for transfers between devices: 28.3 us -> 18.5 us  [body(): terms = lax.all_to_all(terms.reshape(sent.shape), 'inst', 0, 0, tiled=True)]
    pallas_call x1 -> x2, Pallas kernels: 7.88 us -> 9.85 us  [the longest x1 7.58 us: spatial(): pl.pallas_call(spatial_kernel, grid=(count,), out_shape=jax.ShapeDtypeStr...]
    unnamed x8, local copies, waits for them, and re-layouts: 3.07 us -> 1.91 us
  transfers between devices with their start and end apart: 3 -> 3, of which waited for: 2 -> 2; matrix products, arithmetic and copies ran while one was open for 2% -> 2% of each run, Pallas kernels for 0% -> 8%
where the time goes in v3:
time: 95.8 us; the launch traced here: 95.5 us
  blocking collectives  47.5 us (50%)
  waiting for transfers between devices  21.1 us (22%)
  Pallas kernels  12 us (13%)
  starting transfers between devices  8.97 us (9%)
  local copies, waits for them, and re-layouts  5.65 us (6%)
    all_to_all x1, blocking collectives, body(): held = lax.all_to_all(sent, 'inst', 0, 0, tiled=True)  47.5 us
    all_to_all x1, waiting for transfers between devices, body(): terms = lax.all_to_all(terms.reshape(sent.shape), 'inst', 0, 0, tiled=True)  18.5 us
    pallas_call x1, Pallas kernels, spatial(): pl.pallas_call(spatial_kernel, grid=(count,), out_shape=jax.ShapeDtypeStr...  7.58 us
    all_to_all x1, starting transfers between devices, body(): terms = lax.all_to_all(terms.reshape(sent.shape), 'inst', 0, 0, tiled=True)  4.68 us
    ppermute x1, starting transfers between devices, wrap_halos(): lax.ppermute(pack(state[..., :2, :], metrics[0, :, :, :1]), 'wrap', backw...  4.21 us
    ppermute x1, waiting for transfers between devices, wrap_halos(): lax.ppermute(pack(state[..., -2:, :], metrics[0, :, :, -1:]), 'wrap', onw...  2.58 us
    pallas_call x1, Pallas kernels, combined(): pl.pallas_call(combine_kernel, out_shape=jax.ShapeDtypeStruct(local.shape...  2.27 us
    pallas_call x1, Pallas kernels, time_terms(): pl.pallas_call(time_kernel, out_shape=jax.ShapeDtypeStruct(gathered.shape...  2.14 us
  transfers between devices with their start and end apart: 3, of which 2 were waited for; matrix products, arithmetic and copies ran while one was open for 2% of the time, Pallas kernels for 8%

profile of v3, /device:TPU:6, one launch (start us, length us, event | category | flops | bytes accessed | tf_op | source)
XLA Modules:
  0.0 95.5 jit_solution(1235276757216717783)
XLA Ops:
  0.0 1.6 %copy.5 = f32[8,2,2,6,16,128]{5,4,3,2,1,0:T(8,128)S(1)} copy(f32[8,2,2,6,16,128]{5,4,1,0,3,2:T(8,128)} %bitcast.15) | data formatting | bytes 3145728 | tf_op jit(solution)/shard_map/transpose | solution.py:321
  1.6 47.5 %all_to_all.10 = f32[16,192,128]{2,1,0:T(8,128)S(1)} all-to-all(f32[16,192,128]{2,1,0:T(8,128)S(1)} %bitcast.18), channel_id=1, replica_groups=mesh['wrap'=16,'inst'=16] {'inst'}, dimensions={0} | all-to-all | bytes 3145728 | tf_op jit(solution)/shard_map/all_to_all | solution.py:322
  49.2 2.1 %shard_map.38 = f32[32,96,128]{2,1,0:T(8,128)} custom-call(f32[32,96,128]{2,1,0:T(8,128)S(1)} %bitcast.16), custom_call_target="tpu_custom_call" | custom-call | flops 6291456 | bytes 3145728 | tf_op jit(solution)/shard_map/pallas_call | solution.py:90
  51.3 0.0 copy-start
  51.3 4.7 %all-to-all-start.1 = ((f32[16,192,128]{2,1,0:T(8,128)}), f32[16,192,128]{2,1,0:T(8,128)S(1)}, u32[]{:S(2)}, u32[]{:S(2)}) async-start(f32[16,192,128]{2,1,0:T(8,128)} %bitcast.12), calls=%async_computation.1 | async-start | bytes 3145728 | tf_op jit(solution)/shard_map/all_to_all | solution.py:324
  56.0 0.0 copy-start.2
  56.0 1.0 %fusion.1 = (f32[1,3,8,1,128]{4,3,2,1,0:T(1,128)S(1)}, f32[1,3,8,1,128]{4,3,2,1,0:T(1,128)S(1)}) fusion(f32[3,3,8,32,128]{4,3,2,1,0:T(8,128)} %metric_ref.1), kind=kLoop, calls=%fused_computation.4 | loop fusion | bytes 49152 | tf_op jit(solution)/shard_map/slice | solution.py:306
  57.0 0.0 copy-done
  57.0 0.1 fusion
  57.1 0.1 collective-permute-start.1
  57.2 4.2 %collective-permute-start = (f32[216,128]{1,0:T(8,128)S(1)}, f32[216,128]{1,0:T(8,128)S(1)}, u32[]{:S(2)}, u32[]{:S(2)}) collective-permute-start(f32[216,128]{1,0:T(8,128)S(1)} %pad_maximum_fusion.1), channel_id=1, source_target_pairs={{16,0},{32,16},{48,32},{64,48},{80,64},{96,80},{112,96},{128,112},... | collective-permute-start | bytes 331784 | tf_op jit(solution)/shard_map/ppermute | solution.py:306
  61.4 2.6 %collective-permute-done.1 = f32[216,128]{1,0:T(8,128)S(1)} collective-permute-done((f32[216,128]{1,0:T(8,128)S(1)}, f32[216,128]{1,0:T(8,128)S(1)}, u32[]{:S(2)}, u32[]{:S(2)}) %collective-permute-start.1) | collective-permute-done | bytes 110624 | tf_op jit(solution)/shard_map/ppermute | solution.py:305
  64.0 0.0 collective-permute-done
  64.0 0.0 copy-start.3
  64.0 0.6 copy-done.3
  64.7 0.1 concatenate.15.metric_halo_ref
  64.8 0.9 slice.34
  65.7 0.2 pad_maximum_fusion.halo_ref
  65.9 0.0 copy-done.2
  65.9 0.0 copy-start.1
  65.9 1.3 %copy-done.1 = f32[3,3,8,32,128]{4,3,2,1,0:T(8,128)S(1)} copy-done((f32[3,3,8,32,128]{4,3,2,1,0:T(8,128)S(1)}, f32[3,3,8,32,128]{4,3,2,1,0:T(8,128)}, u32[]{:S(2)}) %copy-start.1) | copy-done | bytes 1179672
  67.2 7.6 %shard_map.37.spatial_ref = f32[2,6,8,32,128]{4,3,2,1,0:T(8,128)} custom-call(f32[2,6,8,32,128]{4,3,2,1,0:T(8,128)S(1)} %copy-done, f32[2,6,8,8,128]{4,3,2,1,0:T(8,128)S(1)} %pad_maximum_fusion.halo_ref, f32[3,3,8,32,128]{4,3,2,1,0:T(8,128)S(1)} %copy-done.1, f32[3,8,8,128]{3,2,1,0:T(8,128)S(1)} %concatenate.15.metric_halo_ref, f32[8,32,128]{2,1,0:T(8,128)S(1)} %copy-done.2), custom_call_target="tpu_custom_call" | custom-call | flops 26214400 | bytes 5898240 | tf_op jit(solution)/shard_map/pallas_call | solution.py:218
  74.8 18.5 %all-to-all-done.1 = f32[16,192,128]{2,1,0:T(8,128)S(1)} async-done(((f32[16,192,128]{2,1,0:T(8,128)}), f32[16,192,128]{2,1,0:T(8,128)S(1)}, u32[]{:S(2)}, u32[]{:S(2)}) %all-to-all-start.1) | async-done | bytes 1572896 | tf_op jit(solution)/shard_map/all_to_all | solution.py:324
  93.2 2.3 %shard_map.39 = f32[2,6,8,32,128]{4,3,2,1,0:T(8,128)} custom-call(f32[2,6,8,32,128]{4,3,2,1,0:T(8,128)} %shard_map.37.spatial_ref, f32[8,32,128]{2,1,0:T(8,128)S(1)} %copy-done.2, f32[16,2,6,16,128]{4,3,2,1,0:T(8,128)S(1)} %bitcast.17), custom_call_target="tpu_custom_call", output_to_operand_aliasing={{}: (0, {})} | custom-call | flops 786432 | bytes 4718592 | tf_op jit(solution)/shard_map/pallas_call | solution.py:278
  (5 shorter events, 0.0 us)
Async XLA Ops:
  51.3 5.7 %copy-start = (f32[2,6,8,32,128]{4,3,2,1,0:T(8,128)S(1)}, f32[2,6,8,32,128]{4,3,2,1,0:T(8,128)}, u32[]{:S(2)}) copy-start(f32[2,6,8,32,128]{4,3,2,1,0:T(8,128)} %state_ref.1) | copy-start | bytes 4718596
  51.3 41.9 %all-to-all-start.1 = ((f32[16,192,128]{2,1,0:T(8,128)}), f32[16,192,128]{2,1,0:T(8,128)S(1)}, u32[]{:S(2)}, u32[]{:S(2)}) async-start(f32[16,192,128]{2,1,0:T(8,128)} %bitcast.12), calls=%async_computation.1 | async-start | bytes 3145728 | tf_op jit(solution)/shard_map/all_to_all | solution.py:324
  56.0 9.9 %copy-start.2 = (f32[8,32,128]{2,1,0:T(8,128)S(1)}, f32[8,32,128]{2,1,0:T(8,128)}, u32[]{:S(2)}) copy-start(f32[8,32,128]{2,1,0:T(8,128)} %volume_ref.3) | copy-start | bytes 393220
  57.1 6.9 %collective-permute-start.1 = (f32[216,128]{1,0:T(8,128)S(1)}, f32[216,128]{1,0:T(8,128)S(1)}, u32[]{:S(2)}, u32[]{:S(2)}) collective-permute-start(f32[216,128]{1,0:T(8,128)S(1)} %pad_maximum_fusion.2), channel_id=1, source_target_pairs={{0,16},{16,32},{32,48},{48,64},{64,80},{80,96},{96,112},{112,128},... | collective-permute-start | bytes 331784 | tf_op jit(solution)/shard_map/ppermute | solution.py:305
  57.2 6.8 %collective-permute-start = (f32[216,128]{1,0:T(8,128)S(1)}, f32[216,128]{1,0:T(8,128)S(1)}, u32[]{:S(2)}, u32[]{:S(2)}) collective-permute-start(f32[216,128]{1,0:T(8,128)S(1)} %pad_maximum_fusion.1), channel_id=1, source_target_pairs={{16,0},{32,16},{48,32},{64,48},{80,64},{96,80},{112,96},{128,112},... | collective-permute-start | bytes 331784 | tf_op jit(solution)/shard_map/ppermute | solution.py:306
  64.0 0.6 copy-start.3
  65.9 1.3 %copy-start.1 = (f32[3,3,8,32,128]{4,3,2,1,0:T(8,128)S(1)}, f32[3,3,8,32,128]{4,3,2,1,0:T(8,128)}, u32[]{:S(2)}) copy-start(f32[3,3,8,32,128]{4,3,2,1,0:T(8,128)} %metric_ref.1) | copy-start | bytes 3538948

commit v4 on v3

--- a/solution.py
+++ b/solution.py
@@ -11,6 +11,7 @@
 NT = 32
 NJ = 128
 TILE = 8
+WRITES = 4
 BLOCKS = 2
 
 dissipation = 0.03125
@@ -73,17 +74,25 @@
     return [a + b for a, b in zip(even, odd)] + [a - b for a, b in zip(even, odd)]
 
 
-def time_kernel(state_ref, out_ref):
+def time_kernel(state_ref, out_ref, done_ref, sems):
     row = frequency * kernel_row(NT)
-
-    def step(tile, carry):
-        rows = pl.ds(pl.multiple_of(tile * TILE, TILE), TILE)
-        values = [state_ref[n, rows, :] for n in range(NT)]
-        for n, value in enumerate(circular_sums(values, row)):
-            out_ref[n, rows, :] = value
-        return carry
-
-    lax.fori_loop(0, state_ref.shape[1] // TILE, step, 0)
+    lines = state_ref.shape[1] // WRITES
+    writes = []
+    for b in range(WRITES):
+
+        def step(tile, carry):
+            rows = pl.ds(pl.multiple_of(b * lines + tile * TILE, TILE), TILE)
+            values = [state_ref[n, rows, :] for n in range(NT)]
+            for n, value in enumerate(circular_sums(values, row)):
+                done_ref[n, rows, :] = value
+            return carry
+
+        lax.fori_loop(0, lines // TILE, step, 0)
+        rows = slice(b * lines, (b + 1) * lines)
+        writes.append(pltpu.make_async_copy(done_ref.at[:, rows], out_ref.at[:, rows], sems.at[b]))
+        writes[-1].start()
+    for write in writes:
+        write.wait()
 
 
 def time_terms(gathered):
@@ -91,7 +100,8 @@
         time_kernel,
         out_shape=jax.ShapeDtypeStruct(gathered.shape, jnp.float32),
         in_specs=[pl.BlockSpec(memory_space=pltpu.VMEM)],
-        out_specs=pl.BlockSpec(memory_space=pltpu.VMEM),
+        out_specs=pl.BlockSpec(memory_space=pl.ANY),
+        scratch_shapes=[pltpu.VMEM(gathered.shape, jnp.float32), pltpu.SemaphoreType.DMA((WRITES,))],
         compiler_params=pltpu.CompilerParams(vmem_limit_bytes=16 * 2**20),
         cost_estimate=pl.CostEstimate(
             flops=16 * gathered.size, bytes_accessed=8 * gathered.size, transcendentals=0
@@ -125,6 +135,7 @@
     state_ref, halo_ref, metric_ref, metric_halo_ref, volume_ref, out_ref, prim_ref, span_ref
 ):
     depth, height, width = state_ref.shape[2:]
+    n = pl.program_id(0)
     lane = lax.broadcasted_iota(jnp.int32, (height, width), 1)
     first = lane == 0
     last = lane == width - 1
@@ -135,7 +146,7 @@
     up = lambda x: pltpu.roll(x, rows - 1, 0)
 
     def prepare(k, carry):
-        q = [state_ref[0, v, k] for v in range(6)]
+        q = [state_ref[n, v, k] for v in range(6)]
         speed, pressure, sound = primitives(q)
         for v in range(3):
             prim_ref[v, k] = speed[v]
@@ -154,7 +165,7 @@
         speed = [prim_ref[v, k] for v in range(3)]
         pressure = prim_ref[3, k]
         sound = prim_ref[4, k]
-        halo = [halo_ref[0, v, k] for v in range(6)]
+        halo = [halo_ref[n, v, k] for v in range(6)]
         halo_speed, halo_pressure, halo_sound = primitives(halo)
         join = lambda a, b: jnp.concatenate([a, b], axis=0)
         wrap_normal = [join(metric_ref[0, c, k], metric_halo_ref[c, k]) for c in range(3)]
@@ -171,7 +182,7 @@
         squared = (
             wall_normal[0] * wall_normal[0] + wall_normal[1] * wall_normal[1] + wall_normal[2] * wall_normal[2]
         )
-        coefficient = viscosity * (1.0 + state_ref[0, 5, k]) * (squared / volume)
+        coefficient = viscosity * (1.0 + state_ref[n, 5, k]) * (squared / volume)
         coefficient = coefficient + back(coefficient)
         k1 = jnp.maximum(k - 1, 0)
         k2 = jnp.maximum(k - 2, 0)
@@ -181,7 +192,7 @@
         span_high = dissipation * (span_ref[6, k] + span_ref[6, k3])
 
         for v in range(6):
-            q = state_ref[0, v, k]
+            q = state_ref[n, v, k]
             cells = join(q, halo[v])
             face = flux(v, cells, wrap_speed, wrap_pressure, wrap_normal)
             step_one = cells - down(cells)
@@ -198,14 +209,14 @@
                 face = face - coefficient * step_one
             end = 2.0 * cell - wall_end * step_one
             total = total + (jnp.where(last, end, ahead(face)) - face)
-            q1 = state_ref[0, v, k1]
-            q2 = state_ref[0, v, k2]
-            q3 = state_ref[0, v, k3]
-            q4 = state_ref[0, v, k4]
+            q1 = state_ref[n, v, k1]
+            q2 = state_ref[n, v, k2]
+            q3 = state_ref[n, v, k3]
+            q4 = state_ref[n, v, k4]
             total = total + (span_ref[v, k3] - span_ref[v, k1])
             total = total - span_high * (q4 - q1 - 3.0 * (q3 - q))
             total = total + span_low * (q3 - q2 - 3.0 * (q - q1))
-            out_ref[0, v, k] = 0.5 * total
+            out_ref[n, v, k] = total
         return carry
 
     lax.fori_loop(0, depth, step, 0)
@@ -213,20 +224,13 @@
 
 def spatial(state, halo, metrics, metric_halo, volume):
     count, variables, depth, height, width = state.shape
-    whole = lambda a: pl.BlockSpec(a.shape, lambda n: (0,) * a.ndim)
-    each = lambda a: pl.BlockSpec((1,) + a.shape[1:], lambda n: (n,) + (0,) * (a.ndim - 1))
+    vmem = pl.BlockSpec(memory_space=pltpu.VMEM)
     return pl.pallas_call(
         spatial_kernel,
         grid=(count,),
         out_shape=jax.ShapeDtypeStruct(state.shape, jnp.float32),
-        in_specs=[
-            each(state),
-            each(halo),
-            whole(metrics),
-            whole(metric_halo),
-            whole(volume),
-        ],
-        out_specs=each(state),
+        in_specs=[vmem] * 5,
+        out_specs=vmem,
         scratch_shapes=[
             pltpu.VMEM((5, depth, height, width), jnp.float32),
             pltpu.VMEM((7, depth, height, width), jnp.float32),
@@ -240,29 +244,22 @@
     )(state, halo, metrics, metric_halo, volume)
 
 
-def combine_kernel(spatial_ref, volume_ref, term_ref, out_ref, held_ref, in_sems, out_sems):
+def combine_kernel(spatial_ref, volume_ref, term_ref, out_ref, done_ref, sems):
     count, variables, depth = spatial_ref.shape[:3]
     parts = term_ref.shape[0] // depth
     run = variables // BLOCKS
     blocks = [(n, slice(b * run, (b + 1) * run)) for n in range(count) for b in range(BLOCKS)]
-    fetches = [
-        pltpu.make_async_copy(spatial_ref.at[n, r], held_ref.at[n, r], in_sems.at[b])
+    writes = [
+        pltpu.make_async_copy(done_ref.at[n, r], out_ref.at[n, r], sems.at[b])
         for b, (n, r) in enumerate(blocks)
     ]
-    writes = [
-        pltpu.make_async_copy(held_ref.at[n, r], out_ref.at[n, r], out_sems.at[b])
-        for b, (n, r) in enumerate(blocks)
-    ]
-    for fetch in fetches:
-        fetch.start()
     for b, (n, r) in enumerate(blocks):
-        fetches[b].wait()
 
         def step(k, carry):
             volume = volume_ref[k]
             for v in range(r.start, r.stop):
                 term = jnp.concatenate([term_ref[parts * k + p, n, v] for p in range(parts)], axis=0)
-                held_ref[n, v, k] = held_ref[n, v, k] + volume * term
+                done_ref[n, v, k] = spatial_ref[n, v, k] + volume * term
             return carry
 
         lax.fori_loop(0, depth, step, 0)
@@ -272,19 +269,15 @@
 
 
 def combined(local, volume, terms):
-    count = local.shape[0] * BLOCKS
     vmem = pl.BlockSpec(memory_space=pltpu.VMEM)
-    anywhere = pl.BlockSpec(memory_space=pl.ANY)
     return pl.pallas_call(
         combine_kernel,
         out_shape=jax.ShapeDtypeStruct(local.shape, jnp.float32),
-        in_specs=[anywhere, vmem, vmem],
-        out_specs=anywhere,
-        input_output_aliases={0: 0},
+        in_specs=[vmem] * 3,
+        out_specs=pl.BlockSpec(memory_space=pl.ANY),
         scratch_shapes=[
             pltpu.VMEM(local.shape, jnp.float32),
-            pltpu.SemaphoreType.DMA((count,)),
-            pltpu.SemaphoreType.DMA((count,)),
+            pltpu.SemaphoreType.DMA((local.shape[0] * BLOCKS,)),
         ],
         compiler_params=pltpu.CompilerParams(vmem_limit_bytes=16 * 2**20),
         cost_estimate=pl.CostEstimate(
@@ -324,7 +317,7 @@
     terms = lax.all_to_all(terms.reshape(sent.shape), "inst", 0, 0, tiled=True)
     terms = terms.reshape(owners, inst_count, variables, lines, width)
     local = spatial(state, halo, metrics, metric_halo, volume)
-    return combined(local, volume, terms)
+    return combined(0.5 * local, volume, terms)
 
 
 def solution(mesh):

time: 95.8 us -> 94.4 us (0.985)
  Pallas kernels: 12 us -> 9.66 us
    pallas_call x1, Pallas kernels: 2.27 us -> 1.24 us  [combined(): pl.pallas_call(combine_kernel, out_shape=jax.ShapeDtypeStruct(local.shape...]
  transfers between devices with their start and end apart: 3 -> 3, of which waited for: 2 -> 2; matrix products, arithmetic and copies ran while one was open for 2% -> 3% of each run, Pallas kernels for 8% -> 7%
where the time goes in v4:
time: 94.4 us; the launch traced here: 94.1 us
  blocking collectives  47.5 us (50%)
  waiting for transfers between devices  21.7 us (23%)
  Pallas kernels  9.66 us (10%)
  starting transfers between devices  8.98 us (10%)
  local copies, waits for them, and re-layouts  5.65 us (6%)
    all_to_all x1, blocking collectives, body(): held = lax.all_to_all(sent, 'inst', 0, 0, tiled=True)  47.5 us
    all_to_all x1, waiting for transfers between devices, body(): terms = lax.all_to_all(terms.reshape(sent.shape), 'inst', 0, 0, tiled=True)  19.1 us
    pallas_call x1, Pallas kernels, spatial(): pl.pallas_call(spatial_kernel, grid=(count,), out_shape=jax.ShapeDtypeStr...  6.65 us
    all_to_all x1, starting transfers between devices, body(): terms = lax.all_to_all(terms.reshape(sent.shape), 'inst', 0, 0, tiled=True)  4.69 us
    ppermute x1, starting transfers between devices, wrap_halos(): lax.ppermute(pack(state[..., :2, :], metrics[0, :, :, :1]), 'wrap', backw...  4.21 us
    ppermute x1, waiting for transfers between devices, wrap_halos(): lax.ppermute(pack(state[..., -2:, :], metrics[0, :, :, -1:]), 'wrap', onw...  2.58 us
    unnamed x8, local copies, waits for them, and re-layouts  1.91 us
  transfers between devices with their start and end apart: 3, of which 2 were waited for; matrix products, arithmetic and copies ran while one was open for 3% of the time, Pallas kernels for 7%

profile of v4, /device:TPU:6, one launch (start us, length us, event | category | flops | bytes accessed | tf_op | source)
XLA Modules:
  0.0 94.1 jit_solution(10903711161044316565)
XLA Ops:
  0.0 1.6 %copy.4 = f32[8,2,2,6,16,128]{5,4,3,2,1,0:T(8,128)S(1)} copy(f32[8,2,2,6,16,128]{5,4,1,0,3,2:T(8,128)} %bitcast.15) | data formatting | bytes 3145728 | tf_op jit(solution)/shard_map/transpose | solution.py:314
  1.6 47.5 %all_to_all.10 = f32[16,192,128]{2,1,0:T(8,128)S(1)} all-to-all(f32[16,192,128]{2,1,0:T(8,128)S(1)} %bitcast.18), channel_id=1, replica_groups=mesh['wrap'=16,'inst'=16] {'inst'}, dimensions={0} | all-to-all | bytes 3145728 | tf_op jit(solution)/shard_map/all_to_all | solution.py:315
  49.2 1.8 %shard_map.38 = f32[32,96,128]{2,1,0:T(8,128)} custom-call(f32[32,96,128]{2,1,0:T(8,128)S(1)} %bitcast.16), custom_call_target="tpu_custom_call" | custom-call | flops 6291456 | bytes 3145728 | tf_op jit(solution)/shard_map/pallas_call | solution.py:99
  50.9 0.0 copy-start
  51.0 4.7 %all-to-all-start.1 = ((f32[16,192,128]{2,1,0:T(8,128)}), f32[16,192,128]{2,1,0:T(8,128)S(1)}, u32[]{:S(2)}, u32[]{:S(2)}) async-start(f32[16,192,128]{2,1,0:T(8,128)} %bitcast.12), calls=%async_computation.1 | async-start | bytes 3145728 | tf_op jit(solution)/shard_map/all_to_all | solution.py:317
  55.7 0.0 copy-start.2
  55.7 1.0 %fusion.1 = (f32[1,3,8,1,128]{4,3,2,1,0:T(1,128)S(1)}, f32[1,3,8,1,128]{4,3,2,1,0:T(1,128)S(1)}) fusion(f32[3,3,8,32,128]{4,3,2,1,0:T(8,128)} %metric_ref.1), kind=kLoop, calls=%fused_computation.5 | loop fusion | bytes 49152 | tf_op jit(solution)/shard_map/slice | solution.py:299
  56.7 0.0 copy-done
  56.7 0.1 fusion
  56.8 0.1 collective-permute-start.1
  56.9 4.2 %collective-permute-start = (f32[216,128]{1,0:T(8,128)S(1)}, f32[216,128]{1,0:T(8,128)S(1)}, u32[]{:S(2)}, u32[]{:S(2)}) collective-permute-start(f32[216,128]{1,0:T(8,128)S(1)} %pad_maximum_fusion.1), channel_id=1, source_target_pairs={{16,0},{32,16},{48,32},{64,48},{80,64},{96,80},{112,96},{128,112},... | collective-permute-start | bytes 331784 | tf_op jit(solution)/shard_map/ppermute | solution.py:299
  61.1 2.6 %collective-permute-done.1 = f32[216,128]{1,0:T(8,128)S(1)} collective-permute-done((f32[216,128]{1,0:T(8,128)S(1)}, f32[216,128]{1,0:T(8,128)S(1)}, u32[]{:S(2)}, u32[]{:S(2)}) %collective-permute-start.1) | collective-permute-done | bytes 110624 | tf_op jit(solution)/shard_map/ppermute | solution.py:298
  63.7 0.0 collective-permute-done
  63.7 0.6 copy-done.3
  64.3 0.1 concatenate.15.metric_halo_ref
  64.5 0.9 slice.34
  65.4 0.2 pad_maximum_fusion.halo_ref
  65.6 0.0 copy-done.2
  65.6 0.0 copy-start.1
  65.6 1.3 %copy-done.1 = f32[3,3,8,32,128]{4,3,2,1,0:T(8,128)S(1)} copy-done((f32[3,3,8,32,128]{4,3,2,1,0:T(8,128)S(1)}, f32[3,3,8,32,128]{4,3,2,1,0:T(8,128)}, u32[]{:S(2)}) %copy-start.1) | copy-done | bytes 1179672
  66.8 6.7 %shard_map.37 = f32[2,6,8,32,128]{4,3,2,1,0:T(8,128)S(1)} custom-call(f32[2,6,8,32,128]{4,3,2,1,0:T(8,128)S(1)} %copy-done, f32[2,6,8,8,128]{4,3,2,1,0:T(8,128)S(1)} %pad_maximum_fusion.halo_ref, f32[3,3,8,32,128]{4,3,2,1,0:T(8,128)S(1)} %copy-done.1, f32[3,8,8,128]{3,2,1,0:T(8,128)S(1)} %concatenate.15.metric_halo_ref, f32[8,32,128]{2,1,0:T(8,128)S(1)} %copy-done.2), custom_call_target="tpu_custom_call" | custom-call | flops 26214400 | bytes 5898240 | tf_op jit(solution)/shard_map/pallas_call | solution.py:228
  73.5 0.3 broadcast_multiply_fusion.spatial_ref
  73.8 19.1 %all-to-all-done.1 = f32[16,192,128]{2,1,0:T(8,128)S(1)} async-done(((f32[16,192,128]{2,1,0:T(8,128)}), f32[16,192,128]{2,1,0:T(8,128)S(1)}, u32[]{:S(2)}, u32[]{:S(2)}) %all-to-all-start.1) | async-done | bytes 1572896 | tf_op jit(solution)/shard_map/all_to_all | solution.py:317
  92.9 1.2 %shard_map.39 = f32[2,6,8,32,128]{4,3,2,1,0:T(8,128)} custom-call(f32[2,6,8,32,128]{4,3,2,1,0:T(8,128)S(1)} %broadcast_multiply_fusion.spatial_ref, f32[8,32,128]{2,1,0:T(8,128)S(1)} %copy-done.2, f32[16,2,6,16,128]{4,3,2,1,0:T(8,128)S(1)} %bitcast.17), custom_call_target="tpu_custom_call" | custom-call | flops 786432 | bytes 4718592 | tf_op jit(solution)/shard_map/pallas_call | solution.py:273
  (6 shorter events, 0.0 us)
Async XLA Ops:
  50.9 5.7 %copy-start = (f32[2,6,8,32,128]{4,3,2,1,0:T(8,128)S(1)}, f32[2,6,8,32,128]{4,3,2,1,0:T(8,128)}, u32[]{:S(2)}) copy-start(f32[2,6,8,32,128]{4,3,2,1,0:T(8,128)} %state_ref.1) | copy-start | bytes 4718596
  51.0 41.9 %all-to-all-start.1 = ((f32[16,192,128]{2,1,0:T(8,128)}), f32[16,192,128]{2,1,0:T(8,128)S(1)}, u32[]{:S(2)}, u32[]{:S(2)}) async-start(f32[16,192,128]{2,1,0:T(8,128)} %bitcast.12), calls=%async_computation.1 | async-start | bytes 3145728 | tf_op jit(solution)/shard_map/all_to_all | solution.py:317
  55.7 9.9 %copy-start.2 = (f32[8,32,128]{2,1,0:T(8,128)S(1)}, f32[8,32,128]{2,1,0:T(8,128)}, u32[]{:S(2)}) copy-start(f32[8,32,128]{2,1,0:T(8,128)} %volume_ref.3) | copy-start | bytes 393220
  56.8 6.9 %collective-permute-start.1 = (f32[216,128]{1,0:T(8,128)S(1)}, f32[216,128]{1,0:T(8,128)S(1)}, u32[]{:S(2)}, u32[]{:S(2)}) collective-permute-start(f32[216,128]{1,0:T(8,128)S(1)} %pad_maximum_fusion.2), channel_id=1, source_target_pairs={{0,16},{16,32},{32,48},{48,64},{64,80},{80,96},{96,112},{112,128},... | collective-permute-start | bytes 331784 | tf_op jit(solution)/shard_map/ppermute | solution.py:298
  56.9 6.8 %collective-permute-start = (f32[216,128]{1,0:T(8,128)S(1)}, f32[216,128]{1,0:T(8,128)S(1)}, u32[]{:S(2)}, u32[]{:S(2)}) collective-permute-start(f32[216,128]{1,0:T(8,128)S(1)} %pad_maximum_fusion.1), channel_id=1, source_target_pairs={{16,0},{32,16},{48,32},{64,48},{80,64},{96,80},{112,96},{128,112},... | collective-permute-start | bytes 331784 | tf_op jit(solution)/shard_map/ppermute | solution.py:299
  63.7 0.6 copy-start.3
  65.6 1.3 %copy-start.1 = (f32[3,3,8,32,128]{4,3,2,1,0:T(8,128)S(1)}, f32[3,3,8,32,128]{4,3,2,1,0:T(8,128)}, u32[]{:S(2)}) copy-start(f32[3,3,8,32,128]{4,3,2,1,0:T(8,128)} %metric_ref.1) | copy-start | bytes 3538948

commit v5 on v4

--- a/solution.py
+++ b/solution.py
@@ -1,3 +1,4 @@
+import functools
 import math
 
 import jax
@@ -11,6 +12,9 @@
 NT = 32
 NJ = 128
 TILE = 8
+FIRST = 62
+SECOND = 61
+WRITTEN = (8, 4)
 WRITES = 4
 BLOCKS = 2
 
@@ -74,6 +78,39 @@
     return [a + b for a, b in zip(even, odd)] + [a - b for a, b in zip(even, odd)]
 
 
+def pack_kernel(state_ref, local_ref, sent_ref, sems):
+    count, variables, depth, height, width = state_ref.shape
+    owners, _, _, lines, _ = sent_ref.shape
+    parts = height // lines
+    copies = [
+        pltpu.make_async_copy(
+            state_ref.at[n, :, k, p * lines : (p + 1) * lines],
+            sent_ref.at[parts * k + p, n],
+            sems.at[n, parts * k + p],
+        )
+        for k in range(depth)
+        for p in range(parts)
+        for n in range(count)
+    ]
+    for copy in copies:
+        copy.start()
+    for copy in copies:
+        copy.wait()
+
+
+def packed(state, local, owners):
+    count, variables, depth, height, width = state.shape
+    return pl.pallas_call(
+        pack_kernel,
+        out_shape=pltpu.VMEM((owners, count, variables, height * depth // owners, width), jnp.float32),
+        in_specs=[pl.BlockSpec(memory_space=pl.ANY)] * 2,
+        out_specs=pl.BlockSpec(memory_space=pltpu.VMEM),
+        scratch_shapes=[pltpu.SemaphoreType.DMA((count, owners))],
+        compiler_params=pltpu.CompilerParams(vmem_limit_bytes=61 * 2**20),
+        cost_estimate=pl.CostEstimate(flops=0, bytes_accessed=8 * state.size, transcendentals=0),
+    )(state, local)
+
+
 def time_kernel(state_ref, out_ref, done_ref, sems):
     row = frequency * kernel_row(NT)
     lines = state_ref.shape[1] // WRITES
@@ -131,27 +168,21 @@
     return q * normal_speed
 
 
-def spatial_kernel(
-    state_ref, halo_ref, metric_ref, metric_halo_ref, volume_ref, out_ref, prim_ref, span_ref
-):
+def cross_instance(n, writes, state_ref, metric_ref, volume_ref, out_ref, span_ref, out_hbm, sem):
     depth, height, width = state_ref.shape[2:]
-    n = pl.program_id(0)
     lane = lax.broadcasted_iota(jnp.int32, (height, width), 1)
     first = lane == 0
     last = lane == width - 1
     back = lambda x: pltpu.roll(x, 1, 1)
     ahead = lambda x: pltpu.roll(x, width - 1, 1)
-    rows = height + TILE
-    down = lambda x: pltpu.roll(x, 1, 0)
-    up = lambda x: pltpu.roll(x, rows - 1, 0)
 
     def prepare(k, carry):
         q = [state_ref[n, v, k] for v in range(6)]
         speed, pressure, sound = primitives(q)
         for v in range(3):
-            prim_ref[v, k] = speed[v]
-        prim_ref[3, k] = pressure
-        prim_ref[4, k] = sound
+            span_ref[7 + v, k] = speed[v]
+        span_ref[10, k] = pressure
+        span_ref[11, k] = sound
         normal = [metric_ref[2, c, k] for c in range(3)]
         normal_speed, radius = along(speed, sound, normal)
         span_ref[6, k] = radius
@@ -162,27 +193,17 @@
     lax.fori_loop(0, depth, prepare, 0)
 
     def step(k, carry):
-        speed = [prim_ref[v, k] for v in range(3)]
-        pressure = prim_ref[3, k]
-        sound = prim_ref[4, k]
-        halo = [halo_ref[n, v, k] for v in range(6)]
-        halo_speed, halo_pressure, halo_sound = primitives(halo)
-        join = lambda a, b: jnp.concatenate([a, b], axis=0)
-        wrap_normal = [join(metric_ref[0, c, k], metric_halo_ref[c, k]) for c in range(3)]
-        wrap_pressure = join(pressure, halo_pressure)
-        wrap_speed, wrap_radius = along(
-            [join(a, b) for a, b in zip(speed, halo_speed)], join(sound, halo_sound), wrap_normal
-        )
-        wrap_weight = dissipation * (wrap_radius + down(wrap_radius))
+        speed = [span_ref[7 + v, k] for v in range(3)]
+        pressure = span_ref[10, k]
+        sound = span_ref[11, k]
         wall_normal = [metric_ref[1, c, k] for c in range(3)]
         wall_speed, wall_radius = along(speed, sound, wall_normal)
         wall_weight = dissipation * (wall_radius + jnp.where(first, wall_radius, back(wall_radius)))
         wall_end = (2.0 * dissipation) * wall_radius
-        volume = volume_ref[k]
         squared = (
             wall_normal[0] * wall_normal[0] + wall_normal[1] * wall_normal[1] + wall_normal[2] * wall_normal[2]
         )
-        coefficient = viscosity * (1.0 + state_ref[n, 5, k]) * (squared / volume)
+        coefficient = viscosity * (1.0 + state_ref[n, 5, k]) * (squared / volume_ref[k])
         coefficient = coefficient + back(coefficient)
         k1 = jnp.maximum(k - 1, 0)
         k2 = jnp.maximum(k - 2, 0)
@@ -190,16 +211,8 @@
         k4 = jnp.minimum(k + 2, depth - 1)
         span_low = dissipation * (span_ref[6, k] + span_ref[6, k1])
         span_high = dissipation * (span_ref[6, k] + span_ref[6, k3])
-
         for v in range(6):
             q = state_ref[n, v, k]
-            cells = join(q, halo[v])
-            face = flux(v, cells, wrap_speed, wrap_pressure, wrap_normal)
-            step_one = cells - down(cells)
-            step_two = up(step_one) - step_one
-            step_three = step_two - down(step_two)
-            face = face + down(face) - wrap_weight * step_three
-            total = (up(face) - face)[:height]
             cell = flux(v, q, wall_speed, pressure, wall_normal)
             step_one = jnp.where(first, 0.0, q - back(q))
             step_two = ahead(step_one) - step_one
@@ -208,7 +221,7 @@
             if v > 0:
                 face = face - coefficient * step_one
             end = 2.0 * cell - wall_end * step_one
-            total = total + (jnp.where(last, end, ahead(face)) - face)
+            total = jnp.where(last, end, ahead(face)) - face
             q1 = state_ref[n, v, k1]
             q2 = state_ref[n, v, k2]
             q3 = state_ref[n, v, k3]
@@ -216,44 +229,142 @@
             total = total + (span_ref[v, k3] - span_ref[v, k1])
             total = total - span_high * (q4 - q1 - 3.0 * (q3 - q))
             total = total + span_low * (q3 - q2 - 3.0 * (q - q1))
-            out_ref[n, v, k] = total
+            out_ref[v, k] = total
         return carry
 
-    lax.fori_loop(0, depth, step, 0)
-
-
-def spatial(state, halo, metrics, metric_halo, volume):
+    run = depth // writes
+
+    def write(r, carry):
+        lax.fori_loop(r * run, (r + 1) * run, step, 0)
+        done = pltpu.make_async_copy(
+            out_ref.at[:, pl.ds(r * run, run)], out_hbm.at[n, :, pl.ds(r * run, run)], sem
+        )
+        done.start()
+        done.wait()
+        return carry
+
+    lax.fori_loop(0, writes, write, 0)
+
+
+def cross_kernel(
+    turn, state_hbm, metric_hbm, volume_hbm, out_hbm,
+    state_ref, metric_ref, volume_ref, out_ref, span_ref, in_sems, out_sem,
+):
+    count = state_ref.shape[0]
+
+    @pl.when(lax.axis_index("wrap") % 2 == turn)
+    def _():
+        fetches = [
+            pltpu.make_async_copy(metric_hbm, metric_ref, in_sems.at[0]),
+            pltpu.make_async_copy(volume_hbm, volume_ref, in_sems.at[1]),
+            pltpu.make_async_copy(state_hbm, state_ref, in_sems.at[2]),
+        ]
+        for fetch in fetches:
+            fetch.start()
+        for fetch in fetches:
+            fetch.wait()
+
+        for n in range(count):
+            cross_instance(
+                n, WRITTEN[n % len(WRITTEN)], state_ref, metric_ref, volume_ref, out_ref, span_ref, out_hbm, out_sem
+            )
+
+
+def cross(turn, limit, state, metrics, volume):
     count, variables, depth, height, width = state.shape
-    vmem = pl.BlockSpec(memory_space=pltpu.VMEM)
+    anywhere = pl.BlockSpec(memory_space=pl.ANY)
+    slabs = lambda size: pltpu.VMEM((size, depth, height, width), jnp.float32)
     return pl.pallas_call(
-        spatial_kernel,
-        grid=(count,),
+        functools.partial(cross_kernel, turn),
         out_shape=jax.ShapeDtypeStruct(state.shape, jnp.float32),
-        in_specs=[vmem] * 5,
-        out_specs=vmem,
+        in_specs=[anywhere] * 3,
+        out_specs=anywhere,
         scratch_shapes=[
-            pltpu.VMEM((5, depth, height, width), jnp.float32),
-            pltpu.VMEM((7, depth, height, width), jnp.float32),
+            pltpu.VMEM(state.shape, jnp.float32),
+            pltpu.VMEM(metrics.shape, jnp.float32),
+            pltpu.VMEM(volume.shape, jnp.float32),
+            slabs(variables),
+            slabs(12),
+            pltpu.SemaphoreType.DMA((3,)),
+            pltpu.SemaphoreType.DMA(()),
         ],
-        compiler_params=pltpu.CompilerParams(vmem_limit_bytes=16 * 2**20),
+        compiler_params=pltpu.CompilerParams(vmem_limit_bytes=limit * 2**20),
         cost_estimate=pl.CostEstimate(
-            flops=400 * count * depth * height * width,
+            flops=300 * count * depth * height * width,
             bytes_accessed=12 * state.size + 4 * metrics.size,
             transcendentals=0,
         ),
-    )(state, halo, metrics, metric_halo, volume)
-
-
-def combine_kernel(spatial_ref, volume_ref, term_ref, out_ref, done_ref, sems):
+    )(state, metrics, volume)
+
+
+def wrap_kernel(
+    state_ref, halo_ref, metric_ref, metric_halo_ref, early_hbm, late_hbm, out_ref, cross_ref, sem
+):
+    depth, height, width = state_ref.shape[2:]
+    n = pl.program_id(0)
+    rows = height + TILE
+    down = lambda x: pltpu.roll(x, 1, 0)
+    up = lambda x: pltpu.roll(x, rows - 1, 0)
+    join = lambda a, b: jnp.concatenate([a, b], axis=0)
+    for turn, ref in enumerate([late_hbm, early_hbm]):
+
+        @pl.when(lax.axis_index("wrap") % 2 == turn)
+        def _():
+            fetch = pltpu.make_async_copy(ref.at[n], cross_ref, sem)
+            fetch.start()
+            fetch.wait()
+
+    def step(k, carry):
+        q = [join(state_ref[n, v, k], halo_ref[n, v, k]) for v in range(6)]
+        speed, pressure, sound = primitives(q)
+        normal = [join(metric_ref[0, c, k], metric_halo_ref[c, k]) for c in range(3)]
+        normal_speed, radius = along(speed, sound, normal)
+        weight = dissipation * (radius + down(radius))
+        for v in range(6):
+            face = flux(v, q[v], normal_speed, pressure, normal)
+            step_one = q[v] - down(q[v])
+            step_two = up(step_one) - step_one
+            step_three = step_two - down(step_two)
+            face = face + down(face) - weight * step_three
+            out_ref[n, v, k] = cross_ref[v, k] + (up(face) - face)[:height]
+        return carry
+
+    lax.fori_loop(0, depth, step, 0)
+
+
+def with_wrap(state, halo, metrics, metric_halo, early, late):
+    vmem = pl.BlockSpec(memory_space=pltpu.VMEM)
+    return pl.pallas_call(
+        wrap_kernel,
+        grid=(state.shape[0],),
+        out_shape=jax.ShapeDtypeStruct(state.shape, jnp.float32),
+        in_specs=[vmem] * 4 + [pl.BlockSpec(memory_space=pl.ANY)] * 2,
+        out_specs=vmem,
+        scratch_shapes=[pltpu.VMEM(state.shape[1:], jnp.float32), pltpu.SemaphoreType.DMA(())],
+        compiler_params=pltpu.CompilerParams(vmem_limit_bytes=16 * 2**20),
+        cost_estimate=pl.CostEstimate(
+            flops=30 * state.size, bytes_accessed=12 * state.size + 4 * metrics.size, transcendentals=0
+        ),
+    )(state, halo, metrics, metric_halo, early, late)
+
+
+def combine_kernel(spatial_ref, volume_ref, term_hbm, out_hbm, term_ref, done_ref, in_sems, out_sems):
     count, variables, depth = spatial_ref.shape[:3]
     parts = term_ref.shape[0] // depth
     run = variables // BLOCKS
     blocks = [(n, slice(b * run, (b + 1) * run)) for n in range(count) for b in range(BLOCKS)]
-    writes = [
-        pltpu.make_async_copy(done_ref.at[n, r], out_ref.at[n, r], sems.at[b])
+    fetches = [
+        pltpu.make_async_copy(term_hbm.at[:, n, r], term_ref.at[:, n, r], in_sems.at[b])
         for b, (n, r) in enumerate(blocks)
     ]
+    writes = [
+        pltpu.make_async_copy(done_ref.at[n, r], out_hbm.at[n, r], out_sems.at[b])
+        for b, (n, r) in enumerate(blocks)
+    ]
+    for fetch in fetches:
+        fetch.start()
     for b, (n, r) in enumerate(blocks):
+        fetches[b].wait()
 
         def step(k, carry):
             volume = volume_ref[k]
@@ -270,14 +381,18 @@
 
 def combined(local, volume, terms):
     vmem = pl.BlockSpec(memory_space=pltpu.VMEM)
+    anywhere = pl.BlockSpec(memory_space=pl.ANY)
+    count = local.shape[0] * BLOCKS
     return pl.pallas_call(
         combine_kernel,
         out_shape=jax.ShapeDtypeStruct(local.shape, jnp.float32),
-        in_specs=[vmem] * 3,
-        out_specs=pl.BlockSpec(memory_space=pl.ANY),
+        in_specs=[vmem] * 2 + [anywhere],
+        out_specs=anywhere,
         scratch_shapes=[
+            pltpu.VMEM(terms.shape, jnp.float32),
             pltpu.VMEM(local.shape, jnp.float32),
-            pltpu.SemaphoreType.DMA((local.shape[0] * BLOCKS,)),
+            pltpu.SemaphoreType.DMA((count,)),
+            pltpu.SemaphoreType.DMA((count,)),
         ],
         compiler_params=pltpu.CompilerParams(vmem_limit_bytes=16 * 2**20),
         cost_estimate=pl.CostEstimate(
@@ -309,14 +424,16 @@
     owners = lax.axis_size("inst")
     parts = owners // depth
     lines = height // parts
-    halo, metric_halo = wrap_halos(state, metrics)
-    split = state.reshape(inst_count, variables, depth, parts, lines, width)
-    sent = split.transpose(2, 3, 0, 1, 4, 5).reshape(owners, inst_count * variables * lines, width)
+    early = cross(1, FIRST, state, metrics, volume)
+    sent = packed(state, early, owners).reshape(owners, inst_count * variables * lines, width)
     held = lax.all_to_all(sent, "inst", 0, 0, tiled=True)
     terms = time_terms(held.reshape(owners * inst_count, variables * lines, width))
     terms = lax.all_to_all(terms.reshape(sent.shape), "inst", 0, 0, tiled=True)
     terms = terms.reshape(owners, inst_count, variables, lines, width)
-    local = spatial(state, halo, metrics, metric_halo, volume)
+    late = cross(0, SECOND, state, metrics, volume)
+    after, late = lax.optimization_barrier((state, late))
+    halo, metric_halo = wrap_halos(after, metrics)
+    local = with_wrap(state, halo, metrics, metric_halo, early, late)
     return combined(0.5 * local, volume, terms)
 
 

time: 94.4 us -> 88.7 us (0.940)
  the two profiles are of different devices: /device:TPU:6 before, /device:TPU:1 now
where the time goes in v5:
time: 88.7 us; the launch traced here: 88.3 us
  blocking collectives  34.4 us (39%)
  Pallas kernels  23.5 us (26%)
  waiting for transfers between devices  15.7 us (18%)
  starting transfers between devices  9.36 us (11%)
  local copies, waits for them, and re-layouts  4.75 us (5%)
    all_to_all x1, blocking collectives, body(): held = lax.all_to_all(sent, 'inst', 0, 0, tiled=True)  34.4 us
    pallas_call x2, Pallas kernels, cross(): pl.pallas_call(functools.partial(cross_kernel, turn), out_shape=jax.Shape...  15.6 us
    all_to_all x1, waiting for transfers between devices, body(): terms = lax.all_to_all(terms.reshape(sent.shape), 'inst', 0, 0, tiled=True)  9.26 us
    all_to_all x1, starting transfers between devices, body(): terms = lax.all_to_all(terms.reshape(sent.shape), 'inst', 0, 0, tiled=True)  5.89 us
    unnamed x10, local copies, waits for them, and re-layouts  4.49 us
    ppermute x1, waiting for transfers between devices, wrap_halos(): lax.ppermute(pack(state[..., :2, :], metrics[0, :, :, :1]), 'wrap', backw...  3.41 us
    ppermute x1, waiting for transfers between devices, wrap_halos(): lax.ppermute(pack(state[..., -2:, :], metrics[0, :, :, -1:]), 'wrap', onw...  3.02 us
    ppermute x1, starting transfers between devices, wrap_halos(): lax.ppermute(pack(state[..., -2:, :], metrics[0, :, :, -1:]), 'wrap', onw...  2.6 us
  transfers between devices with their start and end apart: 3, of which 3 were waited for; matrix products, arithmetic and copies ran while one was open for 1% of the time, Pallas kernels for 2%

profile of v5, /device:TPU:1, one launch (start us, length us, event | category | flops | bytes accessed | tf_op | source)
XLA Modules:
  0.0 88.3 jit_solution(8902894919262508992)
XLA Ops:
  0.0 15.5 %shard_map.38.early_hbm.local_ref = f32[2,6,8,32,128]{4,3,2,1,0:T(8,128)} custom-call(f32[2,6,8,32,128]{4,3,2,1,0:T(8,128)} %state_ref.3, f32[3,3,8,32,128]{4,3,2,1,0:T(8,128)} %metric_ref.1, f32[8,32,128]{2,1,0:T(8,128)} %volume_ref.1), custom_call_target="tpu_custom_call" | custom-call | flops 19660800 | bytes 5898240 | tf_op jit(solution)/shard_map/pallas_call | solution.py:277
  15.6 1.7 %shard_map.40 = f32[16,2,6,16,128]{4,3,2,1,0:T(8,128)S(1)} custom-call(f32[2,6,8,32,128]{4,3,2,1,0:T(8,128)} %state_ref.3, f32[2,6,8,32,128]{4,3,2,1,0:T(8,128)} %shard_map.38.early_hbm.local_ref), custom_call_target="tpu_custom_call" | custom-call | bytes 3145728 | tf_op jit(solution)/shard_map/pallas_call | solution.py:103
  17.2 34.4 %all_to_all.10 = f32[16,192,128]{2,1,0:T(8,128)S(1)} all-to-all(f32[16,192,128]{2,1,0:T(8,128)S(1)} %bitcast.13), channel_id=1, replica_groups=mesh['wrap'=16,'inst'=16] {'inst'}, dimensions={0} | all-to-all | bytes 3145728 | tf_op jit(solution)/shard_map/all_to_all | solution.py:429
  51.6 1.8 %shard_map.41 = f32[32,96,128]{2,1,0:T(8,128)} custom-call(f32[32,96,128]{2,1,0:T(8,128)S(1)} %bitcast.12), custom_call_target="tpu_custom_call" | custom-call | flops 6291456 | bytes 3145728 | tf_op jit(solution)/shard_map/pallas_call | solution.py:136
  53.5 5.9 %all-to-all-start.1 = ((f32[16,192,128]{2,1,0:T(8,128)}), f32[16,192,128]{2,1,0:T(8,128)}, u32[]{:S(2)}, u32[]{:S(2)}) async-start(f32[16,192,128]{2,1,0:T(8,128)} %bitcast.10), calls=%async_computation.1 | async-start | bytes 3145728 | tf_op jit(solution)/shard_map/all_to_all | solution.py:431
  59.4 0.0 copy-start.2
  59.4 0.0 copy-start
  59.4 0.1 shard_map.37.late_hbm
  59.5 1.2 %copy-done.2 = f32[3,3,8,32,128]{4,3,2,1,0:T(8,128)S(1)} copy-done((f32[3,3,8,32,128]{4,3,2,1,0:T(8,128)S(1)}, f32[3,3,8,32,128]{4,3,2,1,0:T(8,128)}, u32[]{:S(2)}) %copy-start.2) | copy-done | bytes 1179672
  60.7 0.5 copy-done
  61.1 0.1 fusion
  61.2 0.9 collective-permute-start
  62.1 2.6 %collective-permute-start.1 = (f32[216,128]{1,0:T(8,128)S(1)}, f32[216,128]{1,0:T(8,128)S(1)}, u32[]{:S(2)}, u32[]{:S(2)}) collective-permute-start(f32[216,128]{1,0:T(8,128)S(1)} %pad_maximum_fusion.2), channel_id=1, source_target_pairs={{0,16},{16,32},{32,48},{48,64},{64,80},{80,96},{96,112},{112,128},... | collective-permute-start | bytes 331784 | tf_op jit(solution)/shard_map/ppermute | solution.py:413
  64.7 3.4 %collective-permute-done = f32[216,128]{1,0:T(8,128)S(1)} collective-permute-done((f32[216,128]{1,0:T(8,128)S(1)}, f32[216,128]{1,0:T(8,128)S(1)}, u32[]{:S(2)}, u32[]{:S(2)}) %collective-permute-start) | collective-permute-done | bytes 110624 | tf_op jit(solution)/shard_map/ppermute | solution.py:414
  68.1 3.0 %collective-permute-done.1 = f32[216,128]{1,0:T(8,128)S(1)} collective-permute-done((f32[216,128]{1,0:T(8,128)S(1)}, f32[216,128]{1,0:T(8,128)S(1)}, u32[]{:S(2)}, u32[]{:S(2)}) %collective-permute-start.1) | collective-permute-done | bytes 110624 | tf_op jit(solution)/shard_map/ppermute | solution.py:413
  71.1 0.1 concatenate.15.metric_halo_ref
  71.3 0.2 pad_maximum_fusion.halo_ref
  71.5 0.0 copy-start.1
  71.5 1.4 %copy-done.1 = f32[2,6,8,32,128]{4,3,2,1,0:T(8,128)S(1)} copy-done((f32[2,6,8,32,128]{4,3,2,1,0:T(8,128)S(1)}, f32[2,6,8,32,128]{4,3,2,1,0:T(8,128)}, u32[]{:S(2)}) %copy-start.1) | copy-done | bytes 1572888
  72.9 1.4 %copy-done.3 = f32[2,6,8,32,128]{4,3,2,1,0:T(8,128)S(1)} copy-done((f32[2,6,8,32,128]{4,3,2,1,0:T(8,128)S(1)}, f32[2,6,8,32,128]{4,3,2,1,0:T(8,128)}, u32[]{:S(2)}) %copy-start.3) | copy-done | bytes 1572888
  74.3 2.1 %shard_map.39 = f32[2,6,8,32,128]{4,3,2,1,0:T(8,128)S(1)} custom-call(f32[2,6,8,32,128]{4,3,2,1,0:T(8,128)S(1)} %copy-done, f32[2,6,8,8,128]{4,3,2,1,0:T(8,128)S(1)} %pad_maximum_fusion.halo_ref, f32[3,3,8,32,128]{4,3,2,1,0:T(8,128)S(1)} %copy-done.2, f32[3,8,8,128]{3,2,1,0:T(8,128)S(1)} %concatenate.15.metric_halo_ref, f32[2,6,8,32,128]{4,3,2,1,0:T(8,128)S(1)} %copy-done.1, ...), custom_call_target="tpu_custom_call" | custom-call | flops 11796480 | bytes 5898240 | tf_op jit(solution)/shard_map/pallas_call | solution.py:337
  76.4 0.3 broadcast_multiply_fusion.spatial_ref
  76.7 9.3 %all-to-all-done.1 = f32[16,192,128]{2,1,0:T(8,128)} async-done(((f32[16,192,128]{2,1,0:T(8,128)}), f32[16,192,128]{2,1,0:T(8,128)}, u32[]{:S(2)}, u32[]{:S(2)}) %all-to-all-start.1) | async-done | bytes 1572896 | tf_op jit(solution)/shard_map/all_to_all | solution.py:431
  86.0 2.3 %shard_map.42 = f32[2,6,8,32,128]{4,3,2,1,0:T(8,128)} custom-call(f32[2,6,8,32,128]{4,3,2,1,0:T(8,128)S(1)} %broadcast_multiply_fusion.spatial_ref, f32[8,32,128]{2,1,0:T(8,128)S(1)} %copy-done.4, f32[16,2,6,16,128]{4,3,2,1,0:T(8,128)} %bitcast.11.term_hbm), custom_call_target="tpu_custom_call" | custom-call | flops 786432 | bytes 4718592 | tf_op jit(solution)/shard_map/pallas_call | solution.py:386
  (10 shorter events, 0.1 us)
Async XLA Ops:
  53.5 32.5 %all-to-all-start.1 = ((f32[16,192,128]{2,1,0:T(8,128)}), f32[16,192,128]{2,1,0:T(8,128)}, u32[]{:S(2)}, u32[]{:S(2)}) async-start(f32[16,192,128]{2,1,0:T(8,128)} %bitcast.10), calls=%async_computation.1 | async-start | bytes 3145728 | tf_op jit(solution)/shard_map/all_to_all | solution.py:431
  59.4 1.3 %copy-start.2 = (f32[3,3,8,32,128]{4,3,2,1,0:T(8,128)S(1)}, f32[3,3,8,32,128]{4,3,2,1,0:T(8,128)}, u32[]{:S(2)}) copy-start(f32[3,3,8,32,128]{4,3,2,1,0:T(8,128)} %metric_ref.1) | copy-start | bytes 3538948
  59.4 1.8 %copy-start = (f32[2,6,8,32,128]{4,3,2,1,0:T(8,128)S(1)}, f32[2,6,8,32,128]{4,3,2,1,0:T(8,128)}, u32[]{:S(2)}) copy-start(f32[2,6,8,32,128]{4,3,2,1,0:T(8,128)} %state_ref.3) | copy-start | bytes 4718596
  61.2 6.9 %collective-permute-start = (f32[216,128]{1,0:T(8,128)S(1)}, f32[216,128]{1,0:T(8,128)S(1)}, u32[]{:S(2)}, u32[]{:S(2)}) collective-permute-start(f32[216,128]{1,0:T(8,128)S(1)} %pad_maximum_fusion.1), channel_id=1, source_target_pairs={{16,0},{32,16},{48,32},{64,48},{80,64},{96,80},{112,96},{128,112},... | collective-permute-start | bytes 331784 | tf_op jit(solution)/shard_map/ppermute | solution.py:414
  62.1 9.0 %collective-permute-start.1 = (f32[216,128]{1,0:T(8,128)S(1)}, f32[216,128]{1,0:T(8,128)S(1)}, u32[]{:S(2)}, u32[]{:S(2)}) collective-permute-start(f32[216,128]{1,0:T(8,128)S(1)} %pad_maximum_fusion.2), channel_id=1, source_target_pairs={{0,16},{16,32},{32,48},{48,64},{64,80},{80,96},{96,112},{112,128},... | collective-permute-start | bytes 331784 | tf_op jit(solution)/shard_map/ppermute | solution.py:413
  71.5 1.4 %copy-start.1 = (f32[2,6,8,32,128]{4,3,2,1,0:T(8,128)S(1)}, f32[2,6,8,32,128]{4,3,2,1,0:T(8,128)}, u32[]{:S(2)}) copy-start(f32[2,6,8,32,128]{4,3,2,1,0:T(8,128)} %shard_map.38.early_hbm.local_ref) | copy-start | bytes 4718596
  72.9 1.4 %copy-start.3 = (f32[2,6,8,32,128]{4,3,2,1,0:T(8,128)S(1)}, f32[2,6,8,32,128]{4,3,2,1,0:T(8,128)}, u32[]{:S(2)}) copy-start(f32[2,6,8,32,128]{4,3,2,1,0:T(8,128)} %shard_map.37.late_hbm) | copy-start | bytes 4718596
  76.4 9.6 %copy-start.4 = (f32[8,32,128]{2,1,0:T(8,128)S(1)}, f32[8,32,128]{2,1,0:T(8,128)}, u32[]{:S(2)}) copy-start(f32[8,32,128]{2,1,0:T(8,128)} %volume_ref.1) | copy-start | bytes 393220

commit v6 on v5

--- a/solution.py
+++ b/solution.py
@@ -14,7 +14,8 @@
 TILE = 8
 FIRST = 62
 SECOND = 61
-WRITTEN = (8, 4)
+EARLY = (4, 4)
+LATE = (1, 1)
 WRITES = 4
 BLOCKS = 2
 
@@ -139,7 +140,7 @@
         in_specs=[pl.BlockSpec(memory_space=pltpu.VMEM)],
         out_specs=pl.BlockSpec(memory_space=pl.ANY),
         scratch_shapes=[pltpu.VMEM(gathered.shape, jnp.float32), pltpu.SemaphoreType.DMA((WRITES,))],
-        compiler_params=pltpu.CompilerParams(vmem_limit_bytes=16 * 2**20),
+        compiler_params=pltpu.CompilerParams(vmem_limit_bytes=61 * 2**20),
         cost_estimate=pl.CostEstimate(
             flops=16 * gathered.size, bytes_accessed=8 * gathered.size, transcendentals=0
         ),
@@ -247,7 +248,7 @@
 
 
 def cross_kernel(
-    turn, state_hbm, metric_hbm, volume_hbm, out_hbm,
+    turn, writes, state_hbm, metric_hbm, volume_hbm, out_hbm,
     state_ref, metric_ref, volume_ref, out_ref, span_ref, in_sems, out_sem,
 ):
     count = state_ref.shape[0]
@@ -266,16 +267,16 @@
 
         for n in range(count):
             cross_instance(
-                n, WRITTEN[n % len(WRITTEN)], state_ref, metric_ref, volume_ref, out_ref, span_ref, out_hbm, out_sem
+                n, writes[n % len(writes)], state_ref, metric_ref, volume_ref, out_ref, span_ref, out_hbm, out_sem
             )
 
 
-def cross(turn, limit, state, metrics, volume):
+def cross(turn, writes, limit, state, metrics, volume):
     count, variables, depth, height, width = state.shape
     anywhere = pl.BlockSpec(memory_space=pl.ANY)
     slabs = lambda size: pltpu.VMEM((size, depth, height, width), jnp.float32)
     return pl.pallas_call(
-        functools.partial(cross_kernel, turn),
+        functools.partial(cross_kernel, turn, writes),
         out_shape=jax.ShapeDtypeStruct(state.shape, jnp.float32),
         in_specs=[anywhere] * 3,
         out_specs=anywhere,
@@ -306,7 +307,7 @@
     down = lambda x: pltpu.roll(x, 1, 0)
     up = lambda x: pltpu.roll(x, rows - 1, 0)
     join = lambda a, b: jnp.concatenate([a, b], axis=0)
-    for turn, ref in enumerate([late_hbm, early_hbm]):
+    for turn, ref in enumerate([early_hbm, late_hbm]):
 
         @pl.when(lax.axis_index("wrap") % 2 == turn)
         def _():
@@ -424,13 +425,13 @@
     owners = lax.axis_size("inst")
     parts = owners // depth
     lines = height // parts
-    early = cross(1, FIRST, state, metrics, volume)
+    early = cross(0, EARLY, FIRST, state, metrics, volume)
     sent = packed(state, early, owners).reshape(owners, inst_count * variables * lines, width)
     held = lax.all_to_all(sent, "inst", 0, 0, tiled=True)
     terms = time_terms(held.reshape(owners * inst_count, variables * lines, width))
     terms = lax.all_to_all(terms.reshape(sent.shape), "inst", 0, 0, tiled=True)
     terms = terms.reshape(owners, inst_count, variables, lines, width)
-    late = cross(0, SECOND, state, metrics, volume)
+    late = cross(1, LATE, SECOND, state, metrics, volume)
     after, late = lax.optimization_barrier((state, late))
     halo, metric_halo = wrap_halos(after, metrics)
     local = with_wrap(state, halo, metrics, metric_halo, early, late)

time: 88.7 us -> 85.4 us (0.963)
  the two profiles are of different devices: /device:TPU:1 before, /device:TPU:6 now
where the time goes in v6:
time: 85.4 us; the launch traced here: 84.8 us
  blocking collectives  34.5 us (40%)
  Pallas kernels  22.4 us (26%)
  waiting for transfers between devices  16.2 us (19%)
  starting transfers between devices  6.3 us (7%)
  local copies, waits for them, and re-layouts  4.75 us (6%)
    all_to_all x1, blocking collectives, body(): held = lax.all_to_all(sent, 'inst', 0, 0, tiled=True)  34.5 us
    pallas_call x2, Pallas kernels, cross(): pl.pallas_call(functools.partial(cross_kernel, turn, writes), out_shape=j...  13.2 us
    all_to_all x1, waiting for transfers between devices, body(): terms = lax.all_to_all(terms.reshape(sent.shape), 'inst', 0, 0, tiled=True)  9.09 us
    all_to_all x1, starting transfers between devices, body(): terms = lax.all_to_all(terms.reshape(sent.shape), 'inst', 0, 0, tiled=True)  5.65 us
    ppermute x1, waiting for transfers between devices, wrap_halos(): lax.ppermute(pack(state[..., -2:, :], metrics[0, :, :, -1:]), 'wrap', onw...  5.33 us
    unnamed x10, local copies, waits for them, and re-layouts  4.49 us
    pallas_call x1, Pallas kernels, time_terms(): pl.pallas_call(time_kernel, out_shape=jax.ShapeDtypeStruct(gathered.shape...  3.19 us
    pallas_call x1, Pallas kernels, combined(): pl.pallas_call(combine_kernel, out_shape=jax.ShapeDtypeStruct(local.shape...  2.27 us
  transfers between devices with their start and end apart: 3, of which 3 were waited for; matrix products, arithmetic and copies ran while one was open for 1% of the time, Pallas kernels for 3%

profile of v6, /device:TPU:6, one launch (start us, length us, event | category | flops | bytes accessed | tf_op | source)
XLA Modules:
  0.0 84.8 jit_solution(15499793553284640096)
XLA Ops:
  0.0 13.1 %shard_map.38.early_hbm.local_ref = f32[2,6,8,32,128]{4,3,2,1,0:T(8,128)} custom-call(f32[2,6,8,32,128]{4,3,2,1,0:T(8,128)} %state_ref.3, f32[3,3,8,32,128]{4,3,2,1,0:T(8,128)} %metric_ref.1, f32[8,32,128]{2,1,0:T(8,128)} %volume_ref.1), custom_call_target="tpu_custom_call" | custom-call | flops 19660800 | bytes 5898240 | tf_op jit(solution)/shard_map/pallas_call | solution.py:278
  13.1 1.7 %shard_map.40 = f32[16,2,6,16,128]{4,3,2,1,0:T(8,128)S(1)} custom-call(f32[2,6,8,32,128]{4,3,2,1,0:T(8,128)} %state_ref.3, f32[2,6,8,32,128]{4,3,2,1,0:T(8,128)} %shard_map.38.early_hbm.local_ref), custom_call_target="tpu_custom_call" | custom-call | bytes 3145728 | tf_op jit(solution)/shard_map/pallas_call | solution.py:104
  14.8 34.5 %all_to_all.10 = f32[16,192,128]{2,1,0:T(8,128)} all-to-all(f32[16,192,128]{2,1,0:T(8,128)S(1)} %bitcast.12), channel_id=1, replica_groups=mesh['wrap'=16,'inst'=16] {'inst'}, dimensions={0} | all-to-all | bytes 3145728 | tf_op jit(solution)/shard_map/all_to_all | solution.py:430
  49.3 3.2 %shard_map.41 = f32[32,96,128]{2,1,0:T(8,128)} custom-call(f32[32,96,128]{2,1,0:T(8,128)} %bitcast.14), custom_call_target="tpu_custom_call" | custom-call | flops 6291456 | bytes 3145728 | tf_op jit(solution)/shard_map/pallas_call | solution.py:137
  52.5 5.6 %all-to-all-start.1 = ((f32[16,192,128]{2,1,0:T(8,128)}), f32[16,192,128]{2,1,0:T(8,128)}, u32[]{:S(2)}, u32[]{:S(2)}) async-start(f32[16,192,128]{2,1,0:T(8,128)} %bitcast.13), calls=%async_computation.1 | async-start | bytes 3145728 | tf_op jit(solution)/shard_map/all_to_all | solution.py:432
  58.2 0.0 copy-start.2
  58.2 0.0 copy-start
  58.2 0.1 shard_map.37.late_hbm
  58.3 1.2 %copy-done.2 = f32[3,3,8,32,128]{4,3,2,1,0:T(8,128)S(1)} copy-done((f32[3,3,8,32,128]{4,3,2,1,0:T(8,128)S(1)}, f32[3,3,8,32,128]{4,3,2,1,0:T(8,128)}, u32[]{:S(2)}) %copy-start.2) | copy-done | bytes 1179672
  59.5 0.5 copy-done
  60.0 0.1 fusion
  60.1 0.1 collective-permute-start
  60.2 0.6 collective-permute-start.1
  60.7 1.7 %collective-permute-done = f32[216,128]{1,0:T(8,128)S(1)} collective-permute-done((f32[216,128]{1,0:T(8,128)S(1)}, f32[216,128]{1,0:T(8,128)S(1)}, u32[]{:S(2)}, u32[]{:S(2)}) %collective-permute-start) | collective-permute-done | bytes 110624 | tf_op jit(solution)/shard_map/ppermute | solution.py:415
  62.5 5.3 %collective-permute-done.1 = f32[216,128]{1,0:T(8,128)S(1)} collective-permute-done((f32[216,128]{1,0:T(8,128)S(1)}, f32[216,128]{1,0:T(8,128)S(1)}, u32[]{:S(2)}, u32[]{:S(2)}) %collective-permute-start.1) | collective-permute-done | bytes 110624 | tf_op jit(solution)/shard_map/ppermute | solution.py:414
  67.8 0.1 concatenate.15.metric_halo_ref
  68.0 0.2 pad_maximum_fusion.halo_ref
  68.2 0.0 copy-start.1
  68.2 1.4 %copy-done.1 = f32[2,6,8,32,128]{4,3,2,1,0:T(8,128)S(1)} copy-done((f32[2,6,8,32,128]{4,3,2,1,0:T(8,128)S(1)}, f32[2,6,8,32,128]{4,3,2,1,0:T(8,128)}, u32[]{:S(2)}) %copy-start.1) | copy-done | bytes 1572888
  69.6 1.4 %copy-done.3 = f32[2,6,8,32,128]{4,3,2,1,0:T(8,128)S(1)} copy-done((f32[2,6,8,32,128]{4,3,2,1,0:T(8,128)S(1)}, f32[2,6,8,32,128]{4,3,2,1,0:T(8,128)}, u32[]{:S(2)}) %copy-start.3) | copy-done | bytes 1572888
  71.0 2.1 %shard_map.39 = f32[2,6,8,32,128]{4,3,2,1,0:T(8,128)S(1)} custom-call(f32[2,6,8,32,128]{4,3,2,1,0:T(8,128)S(1)} %copy-done, f32[2,6,8,8,128]{4,3,2,1,0:T(8,128)S(1)} %pad_maximum_fusion.halo_ref, f32[3,3,8,32,128]{4,3,2,1,0:T(8,128)S(1)} %copy-done.2, f32[3,8,8,128]{3,2,1,0:T(8,128)S(1)} %concatenate.15.metric_halo_ref, f32[2,6,8,32,128]{4,3,2,1,0:T(8,128)S(1)} %copy-done.1, ...), custom_call_target="tpu_custom_call" | custom-call | flops 11796480 | bytes 5898240 | tf_op jit(solution)/shard_map/pallas_call | solution.py:338
  73.1 0.3 broadcast_multiply_fusion.spatial_ref
  73.4 9.1 %all-to-all-done.1 = f32[16,192,128]{2,1,0:T(8,128)} async-done(((f32[16,192,128]{2,1,0:T(8,128)}), f32[16,192,128]{2,1,0:T(8,128)}, u32[]{:S(2)}, u32[]{:S(2)}) %all-to-all-start.1) | async-done | bytes 1572896 | tf_op jit(solution)/shard_map/all_to_all | solution.py:432
  82.5 2.3 %shard_map.42 = f32[2,6,8,32,128]{4,3,2,1,0:T(8,128)} custom-call(f32[2,6,8,32,128]{4,3,2,1,0:T(8,128)S(1)} %broadcast_multiply_fusion.spatial_ref, f32[8,32,128]{2,1,0:T(8,128)S(1)} %copy-done.4, f32[16,2,6,16,128]{4,3,2,1,0:T(8,128)} %bitcast.11.term_hbm), custom_call_target="tpu_custom_call" | custom-call | flops 786432 | bytes 4718592 | tf_op jit(solution)/shard_map/pallas_call | solution.py:387
  (10 shorter events, 0.1 us)
Async XLA Ops:
  52.5 30.0 %all-to-all-start.1 = ((f32[16,192,128]{2,1,0:T(8,128)}), f32[16,192,128]{2,1,0:T(8,128)}, u32[]{:S(2)}, u32[]{:S(2)}) async-start(f32[16,192,128]{2,1,0:T(8,128)} %bitcast.13), calls=%async_computation.1 | async-start | bytes 3145728 | tf_op jit(solution)/shard_map/all_to_all | solution.py:432
  58.2 1.3 %copy-start.2 = (f32[3,3,8,32,128]{4,3,2,1,0:T(8,128)S(1)}, f32[3,3,8,32,128]{4,3,2,1,0:T(8,128)}, u32[]{:S(2)}) copy-start(f32[3,3,8,32,128]{4,3,2,1,0:T(8,128)} %metric_ref.1) | copy-start | bytes 3538948
  58.2 1.8 %copy-start = (f32[2,6,8,32,128]{4,3,2,1,0:T(8,128)S(1)}, f32[2,6,8,32,128]{4,3,2,1,0:T(8,128)}, u32[]{:S(2)}) copy-start(f32[2,6,8,32,128]{4,3,2,1,0:T(8,128)} %state_ref.3) | copy-start | bytes 4718596
  60.1 2.4 %collective-permute-start = (f32[216,128]{1,0:T(8,128)S(1)}, f32[216,128]{1,0:T(8,128)S(1)}, u32[]{:S(2)}, u32[]{:S(2)}) collective-permute-start(f32[216,128]{1,0:T(8,128)S(1)} %pad_maximum_fusion.1), channel_id=1, source_target_pairs={{16,0},{32,16},{48,32},{64,48},{80,64},{96,80},{112,96},{128,112},... | collective-permute-start | bytes 331784 | tf_op jit(solution)/shard_map/ppermute | solution.py:415
  60.2 7.6 %collective-permute-start.1 = (f32[216,128]{1,0:T(8,128)S(1)}, f32[216,128]{1,0:T(8,128)S(1)}, u32[]{:S(2)}, u32[]{:S(2)}) collective-permute-start(f32[216,128]{1,0:T(8,128)S(1)} %pad_maximum_fusion.2), channel_id=1, source_target_pairs={{0,16},{16,32},{32,48},{48,64},{64,80},{80,96},{96,112},{112,128},... | collective-permute-start | bytes 331784 | tf_op jit(solution)/shard_map/ppermute | solution.py:414
  68.2 1.4 %copy-start.1 = (f32[2,6,8,32,128]{4,3,2,1,0:T(8,128)S(1)}, f32[2,6,8,32,128]{4,3,2,1,0:T(8,128)}, u32[]{:S(2)}) copy-start(f32[2,6,8,32,128]{4,3,2,1,0:T(8,128)} %shard_map.38.early_hbm.local_ref) | copy-start | bytes 4718596
  69.6 1.4 %copy-start.3 = (f32[2,6,8,32,128]{4,3,2,1,0:T(8,128)S(1)}, f32[2,6,8,32,128]{4,3,2,1,0:T(8,128)}, u32[]{:S(2)}) copy-start(f32[2,6,8,32,128]{4,3,2,1,0:T(8,128)} %shard_map.37.late_hbm) | copy-start | bytes 4718596
  73.1 9.4 %copy-start.4 = (f32[8,32,128]{2,1,0:T(8,128)S(1)}, f32[8,32,128]{2,1,0:T(8,128)}, u32[]{:S(2)}) copy-start(f32[8,32,128]{2,1,0:T(8,128)} %volume_ref.1) | copy-start | bytes 393220

commit v7 on v6

--- a/solution.py
+++ b/solution.py
@@ -14,9 +14,9 @@
 TILE = 8
 FIRST = 62
 SECOND = 61
-EARLY = (4, 4)
+EARLY = (4, 2)
 LATE = (1, 1)
-WRITES = 4
+WRITES = 6
 BLOCKS = 2
 
 dissipation = 0.03125
@@ -112,35 +112,49 @@
     )(state, local)
 
 
-def time_kernel(state_ref, out_ref, done_ref, sems):
+def time_kernel(gathered_hbm, out_hbm, gathered_ref, done_ref, in_sems, out_sems):
     row = frequency * kernel_row(NT)
-    lines = state_ref.shape[1] // WRITES
-    writes = []
+    lines = gathered_ref.shape[1] // WRITES
+    rows = [slice(b * lines, (b + 1) * lines) for b in range(WRITES)]
+    fetches = [
+        pltpu.make_async_copy(gathered_hbm.at[:, r], gathered_ref.at[:, r], in_sems.at[b])
+        for b, r in enumerate(rows)
+    ]
+    writes = [
+        pltpu.make_async_copy(done_ref.at[:, r], out_hbm.at[:, r], out_sems.at[b]) for b, r in enumerate(rows)
+    ]
+    for fetch in fetches:
+        fetch.start()
     for b in range(WRITES):
+        fetches[b].wait()
 
         def step(tile, carry):
-            rows = pl.ds(pl.multiple_of(b * lines + tile * TILE, TILE), TILE)
-            values = [state_ref[n, rows, :] for n in range(NT)]
+            at = pl.ds(pl.multiple_of(b * lines + tile * TILE, TILE), TILE)
+            values = [gathered_ref[n, at, :] for n in range(NT)]
             for n, value in enumerate(circular_sums(values, row)):
-                done_ref[n, rows, :] = value
+                done_ref[n, at, :] = value
             return carry
 
         lax.fori_loop(0, lines // TILE, step, 0)
-        rows = slice(b * lines, (b + 1) * lines)
-        writes.append(pltpu.make_async_copy(done_ref.at[:, rows], out_ref.at[:, rows], sems.at[b]))
-        writes[-1].start()
+        writes[b].start()
     for write in writes:
         write.wait()
 
 
 def time_terms(gathered):
+    anywhere = pl.BlockSpec(memory_space=pl.ANY)
     return pl.pallas_call(
         time_kernel,
         out_shape=jax.ShapeDtypeStruct(gathered.shape, jnp.float32),
-        in_specs=[pl.BlockSpec(memory_space=pltpu.VMEM)],
-        out_specs=pl.BlockSpec(memory_space=pl.ANY),
-        scratch_shapes=[pltpu.VMEM(gathered.shape, jnp.float32), pltpu.SemaphoreType.DMA((WRITES,))],
-        compiler_params=pltpu.CompilerParams(vmem_limit_bytes=61 * 2**20),
+        in_specs=[anywhere],
+        out_specs=anywhere,
+        scratch_shapes=[
+            pltpu.VMEM(gathered.shape, jnp.float32),
+            pltpu.VMEM(gathered.shape, jnp.float32),
+            pltpu.SemaphoreType.DMA((WRITES,)),
+            pltpu.SemaphoreType.DMA((WRITES,)),
+        ],
+        compiler_params=pltpu.CompilerParams(vmem_limit_bytes=62 * 2**20),
         cost_estimate=pl.CostEstimate(
             flops=16 * gathered.size, bytes_accessed=8 * gathered.size, transcendentals=0
         ),

time: 85.4 us -> 85.9 us (level)
  blocking collectives: 34.5 us -> 36.1 us
  Pallas kernels: 22.4 us -> 20.8 us
    all_to_all x1, blocking collectives: 34.5 us -> 36.1 us  [body(): held = lax.all_to_all(sent, 'inst', 0, 0, tiled=True)]
    pallas_call x2, Pallas kernels: 13.2 us -> 12 us  [cross(): pl.pallas_call(functools.partial(cross_kernel, turn, writes), out_shape=j...]
where the time goes in v7:
time: 85.9 us; the launch traced here: 85.1 us
  blocking collectives  36.1 us (42%)
  Pallas kernels  20.8 us (24%)
  waiting for transfers between devices  16.6 us (19%)
  starting transfers between devices  6.24 us (7%)
  local copies, waits for them, and re-layouts  4.75 us (6%)
    all_to_all x1, blocking collectives, body(): held = lax.all_to_all(sent, 'inst', 0, 0, tiled=True)  36.1 us
    pallas_call x2, Pallas kernels, cross(): pl.pallas_call(functools.partial(cross_kernel, turn, writes), out_shape=j...  12 us
    all_to_all x1, waiting for transfers between devices, body(): terms = lax.all_to_all(terms.reshape(sent.shape), 'inst', 0, 0, tiled=True)  9.36 us
    all_to_all x1, starting transfers between devices, body(): terms = lax.all_to_all(terms.reshape(sent.shape), 'inst', 0, 0, tiled=True)  5.58 us
    ppermute x1, waiting for transfers between devices, wrap_halos(): lax.ppermute(pack(state[..., -2:, :], metrics[0, :, :, -1:]), 'wrap', onw...  5.48 us
    unnamed x10, local copies, waits for them, and re-layouts  4.49 us
    pallas_call x1, Pallas kernels, time_terms(): pl.pallas_call(time_kernel, out_shape=jax.ShapeDtypeStruct(gathered.shape...  2.81 us
    pallas_call x1, Pallas kernels, combined(): pl.pallas_call(combine_kernel, out_shape=jax.ShapeDtypeStruct(local.shape...  2.27 us
  transfers between devices with their start and end apart: 3, of which 3 were waited for; matrix products, arithmetic and copies ran while one was open for 1% of the time, Pallas kernels for 3%

profile of v7, /device:TPU:6, one launch (start us, length us, event | category | flops | bytes accessed | tf_op | source)
XLA Modules:
  0.0 85.1 jit_solution(10942576216602059733)
XLA Ops:
  0.0 11.9 %shard_map.38.early_hbm.local_ref = f32[2,6,8,32,128]{4,3,2,1,0:T(8,128)} custom-call(f32[2,6,8,32,128]{4,3,2,1,0:T(8,128)} %state_ref.3, f32[3,3,8,32,128]{4,3,2,1,0:T(8,128)} %metric_ref.1, f32[8,32,128]{2,1,0:T(8,128)} %volume_ref.1), custom_call_target="tpu_custom_call" | custom-call | flops 19660800 | bytes 5898240 | tf_op jit(solution)/shard_map/pallas_call | solution.py:292
  11.9 1.7 %shard_map.40 = f32[16,2,6,16,128]{4,3,2,1,0:T(8,128)S(1)} custom-call(f32[2,6,8,32,128]{4,3,2,1,0:T(8,128)} %state_ref.3, f32[2,6,8,32,128]{4,3,2,1,0:T(8,128)} %shard_map.38.early_hbm.local_ref), custom_call_target="tpu_custom_call" | custom-call | bytes 3145728 | tf_op jit(solution)/shard_map/pallas_call | solution.py:104
  13.6 36.1 %all_to_all.10 = f32[16,192,128]{2,1,0:T(8,128)} all-to-all(f32[16,192,128]{2,1,0:T(8,128)S(1)} %bitcast.12), channel_id=1, replica_groups=mesh['wrap'=16,'inst'=16] {'inst'}, dimensions={0} | all-to-all | bytes 3145728 | tf_op jit(solution)/shard_map/all_to_all | solution.py:444
  49.7 2.8 %shard_map.41 = f32[32,96,128]{2,1,0:T(8,128)} custom-call(f32[32,96,128]{2,1,0:T(8,128)} %bitcast.14), custom_call_target="tpu_custom_call" | custom-call | flops 6291456 | bytes 3145728 | tf_op jit(solution)/shard_map/pallas_call | solution.py:146
  52.5 5.6 %all-to-all-start.1 = ((f32[16,192,128]{2,1,0:T(8,128)}), f32[16,192,128]{2,1,0:T(8,128)}, u32[]{:S(2)}, u32[]{:S(2)}) async-start(f32[16,192,128]{2,1,0:T(8,128)} %bitcast.13), calls=%async_computation.1 | async-start | bytes 3145728 | tf_op jit(solution)/shard_map/all_to_all | solution.py:446
  58.1 0.0 copy-start.2
  58.1 0.0 copy-start
  58.1 0.1 shard_map.37.late_hbm
  58.2 1.2 %copy-done.2 = f32[3,3,8,32,128]{4,3,2,1,0:T(8,128)S(1)} copy-done((f32[3,3,8,32,128]{4,3,2,1,0:T(8,128)S(1)}, f32[3,3,8,32,128]{4,3,2,1,0:T(8,128)}, u32[]{:S(2)}) %copy-start.2) | copy-done | bytes 1179672
  59.4 0.5 copy-done
  59.9 0.1 fusion
  60.0 0.1 collective-permute-start
  60.1 0.6 collective-permute-start.1
  60.6 1.7 %collective-permute-done = f32[216,128]{1,0:T(8,128)S(1)} collective-permute-done((f32[216,128]{1,0:T(8,128)S(1)}, f32[216,128]{1,0:T(8,128)S(1)}, u32[]{:S(2)}, u32[]{:S(2)}) %collective-permute-start) | collective-permute-done | bytes 110624 | tf_op jit(solution)/shard_map/ppermute | solution.py:429
  62.4 5.5 %collective-permute-done.1 = f32[216,128]{1,0:T(8,128)S(1)} collective-permute-done((f32[216,128]{1,0:T(8,128)S(1)}, f32[216,128]{1,0:T(8,128)S(1)}, u32[]{:S(2)}, u32[]{:S(2)}) %collective-permute-start.1) | collective-permute-done | bytes 110624 | tf_op jit(solution)/shard_map/ppermute | solution.py:428
  67.9 0.1 concatenate.15.metric_halo_ref
  68.0 0.2 pad_maximum_fusion.halo_ref
  68.2 0.0 copy-start.1
  68.2 1.4 %copy-done.1 = f32[2,6,8,32,128]{4,3,2,1,0:T(8,128)S(1)} copy-done((f32[2,6,8,32,128]{4,3,2,1,0:T(8,128)S(1)}, f32[2,6,8,32,128]{4,3,2,1,0:T(8,128)}, u32[]{:S(2)}) %copy-start.1) | copy-done | bytes 1572888
  69.6 1.4 %copy-done.3 = f32[2,6,8,32,128]{4,3,2,1,0:T(8,128)S(1)} copy-done((f32[2,6,8,32,128]{4,3,2,1,0:T(8,128)S(1)}, f32[2,6,8,32,128]{4,3,2,1,0:T(8,128)}, u32[]{:S(2)}) %copy-start.3) | copy-done | bytes 1572888
  71.0 2.1 %shard_map.39 = f32[2,6,8,32,128]{4,3,2,1,0:T(8,128)S(1)} custom-call(f32[2,6,8,32,128]{4,3,2,1,0:T(8,128)S(1)} %copy-done, f32[2,6,8,8,128]{4,3,2,1,0:T(8,128)S(1)} %pad_maximum_fusion.halo_ref, f32[3,3,8,32,128]{4,3,2,1,0:T(8,128)S(1)} %copy-done.2, f32[3,8,8,128]{3,2,1,0:T(8,128)S(1)} %concatenate.15.metric_halo_ref, f32[2,6,8,32,128]{4,3,2,1,0:T(8,128)S(1)} %copy-done.1, ...), custom_call_target="tpu_custom_call" | custom-call | flops 11796480 | bytes 5898240 | tf_op jit(solution)/shard_map/pallas_call | solution.py:352
  73.2 0.3 broadcast_multiply_fusion.spatial_ref
  73.4 9.4 %all-to-all-done.1 = f32[16,192,128]{2,1,0:T(8,128)} async-done(((f32[16,192,128]{2,1,0:T(8,128)}), f32[16,192,128]{2,1,0:T(8,128)}, u32[]{:S(2)}, u32[]{:S(2)}) %all-to-all-start.1) | async-done | bytes 1572896 | tf_op jit(solution)/shard_map/all_to_all | solution.py:446
  82.8 2.3 %shard_map.42 = f32[2,6,8,32,128]{4,3,2,1,0:T(8,128)} custom-call(f32[2,6,8,32,128]{4,3,2,1,0:T(8,128)S(1)} %broadcast_multiply_fusion.spatial_ref, f32[8,32,128]{2,1,0:T(8,128)S(1)} %copy-done.4, f32[16,2,6,16,128]{4,3,2,1,0:T(8,128)} %bitcast.11.term_hbm), custom_call_target="tpu_custom_call" | custom-call | flops 786432 | bytes 4718592 | tf_op jit(solution)/shard_map/pallas_call | solution.py:401
  (10 shorter events, 0.1 us)
Async XLA Ops:
  52.5 30.3 %all-to-all-start.1 = ((f32[16,192,128]{2,1,0:T(8,128)}), f32[16,192,128]{2,1,0:T(8,128)}, u32[]{:S(2)}, u32[]{:S(2)}) async-start(f32[16,192,128]{2,1,0:T(8,128)} %bitcast.13), calls=%async_computation.1 | async-start | bytes 3145728 | tf_op jit(solution)/shard_map/all_to_all | solution.py:446
  58.1 1.3 %copy-start.2 = (f32[3,3,8,32,128]{4,3,2,1,0:T(8,128)S(1)}, f32[3,3,8,32,128]{4,3,2,1,0:T(8,128)}, u32[]{:S(2)}) copy-start(f32[3,3,8,32,128]{4,3,2,1,0:T(8,128)} %metric_ref.1) | copy-start | bytes 3538948
  58.1 1.8 %copy-start = (f32[2,6,8,32,128]{4,3,2,1,0:T(8,128)S(1)}, f32[2,6,8,32,128]{4,3,2,1,0:T(8,128)}, u32[]{:S(2)}) copy-start(f32[2,6,8,32,128]{4,3,2,1,0:T(8,128)} %state_ref.3) | copy-start | bytes 4718596
  60.0 2.4 %collective-permute-start = (f32[216,128]{1,0:T(8,128)S(1)}, f32[216,128]{1,0:T(8,128)S(1)}, u32[]{:S(2)}, u32[]{:S(2)}) collective-permute-start(f32[216,128]{1,0:T(8,128)S(1)} %pad_maximum_fusion.1), channel_id=1, source_target_pairs={{16,0},{32,16},{48,32},{64,48},{80,64},{96,80},{112,96},{128,112},... | collective-permute-start | bytes 331784 | tf_op jit(solution)/shard_map/ppermute | solution.py:429
  60.1 7.8 %collective-permute-start.1 = (f32[216,128]{1,0:T(8,128)S(1)}, f32[216,128]{1,0:T(8,128)S(1)}, u32[]{:S(2)}, u32[]{:S(2)}) collective-permute-start(f32[216,128]{1,0:T(8,128)S(1)} %pad_maximum_fusion.2), channel_id=1, source_target_pairs={{0,16},{16,32},{32,48},{48,64},{64,80},{80,96},{96,112},{112,128},... | collective-permute-start | bytes 331784 | tf_op jit(solution)/shard_map/ppermute | solution.py:428
  68.2 1.4 %copy-start.1 = (f32[2,6,8,32,128]{4,3,2,1,0:T(8,128)S(1)}, f32[2,6,8,32,128]{4,3,2,1,0:T(8,128)}, u32[]{:S(2)}) copy-start(f32[2,6,8,32,128]{4,3,2,1,0:T(8,128)} %shard_map.38.early_hbm.local_ref) | copy-start | bytes 4718596
  69.6 1.4 %copy-start.3 = (f32[2,6,8,32,128]{4,3,2,1,0:T(8,128)S(1)}, f32[2,6,8,32,128]{4,3,2,1,0:T(8,128)}, u32[]{:S(2)}) copy-start(f32[2,6,8,32,128]{4,3,2,1,0:T(8,128)} %shard_map.37.late_hbm) | copy-start | bytes 4718596
  73.1 9.7 %copy-start.4 = (f32[8,32,128]{2,1,0:T(8,128)S(1)}, f32[8,32,128]{2,1,0:T(8,128)}, u32[]{:S(2)}) copy-start(f32[8,32,128]{2,1,0:T(8,128)} %volume_ref.1) | copy-start | bytes 393220
